TPU v7x, 32 devices: a whole 2x2x4 slice. The times are simulated.
32 devices in a mesh: stream: 2 (over x), dp: 16 (over z, y, core).
Axes of the slice: x: 2, y: 2, z: 4, core: 2. Of those that a mesh axis runs over, the one named last changes fastest.
Arguments:
- short_tokens: bfloat16 [2, 128, 32, 512], P('stream', 'dp'), may hold values from -6 to 6
- long_tokens: bfloat16 [2, 128, 128, 512], P('stream', 'dp'), may hold values from -6 to 6
- short_len: int32 [2, 128], P('stream', 'dp'), may hold values from 2 to 32, as said below
- long_len: int32 [2, 128], P('stream', 'dp'), may hold values from 33 to 128, as said below
- pair_index: int32 [256], replicated, may hold values from 0 to 255, each once
- w_qkv: bfloat16 [2, 512, 1536], replicated, may hold values from -0.25 to 0.25
- b_qv: float32 [2, 1024], replicated, may hold values from -1.8 to 1.8
- w_out: bfloat16 [2, 512, 512], replicated, may hold values from -1 to 1
- b_resid: float32 [2, 1024], replicated, may hold values from -1.8 to 1.8
- norm_gain: float32 [2, 1024], replicated, may hold values from 0.5 to 1.5
- norm_bias: float32 [2, 1024], replicated, may hold values from -1.8 to 1.8
- w_in: bfloat16 [2, 512, 2048], replicated, may hold values from -0.25 to 0.25
- b_in: float32 [2, 2048], replicated, may hold values from -1.8 to 1.8
- w_back: bfloat16 [2, 2048, 512], replicated, may hold values from -0.125 to 0.125
Outputs:
- grad_w_qkv: float32 [2, 512, 1536], replicated
- grad_b_qv: float32 [2, 1024], replicated
- grad_w_out: float32 [2, 512, 512], replicated
- grad_b_resid: float32 [2, 1024], replicated
- grad_norm_gain: float32 [2, 1024], replicated
- grad_norm_bias: float32 [2, 1024], replicated
- grad_w_in: float32 [2, 512, 2048], replicated
- grad_b_in: float32 [2, 2048], replicated
- grad_w_back: float32 [2, 2048, 512], replicated
- grad_short: float32 [2, 128, 32, 512], P('stream', 'dp')
- grad_long: float32 [2, 128, 128, 512], P('stream', 'dp')
Inputs may be any that keep to these rules, and one draw needn't show every extreme that they name: `short_len`: lengths in the short bucket; the first short sentence of every data device has all 32 tokens. `long_len`: lengths in the long bucket; on each side some long sentence has all 128 tokens. A permutation: source sentence i and target sentence pair_index[i] are translations; on either side sentences are numbered data device by data device, on each its 8 short ones and then its 8 long ones.
All inputs are finite; a program needn't handle non-finite values.
Results may differ from a plain program's by a relative error of at most 0.023.
Values may be sent and summed in bfloat16 or wider, within the bound.
No kernel may reach another device: no remote copies, remote signals or barrier semaphores. Data moves between devices by JAX's collectives and lax.ppermute only.
A program may use at most 192 MiB of HBM per device.

v0:
```python
import functools
import math

import jax
import jax.numpy as jnp
from jax import lax
from jax.experimental import pallas as pl
from jax.experimental.pallas import tpu as pltpu
from jax.sharding import PartitionSpec as P

HEADS = 8
BF = jnp.bfloat16
F32 = jnp.float32
AXES = ("stream", "dp")
logit_scale = 40.0
margin = 0.3
norm_eps = 1e-12
unit_eps = 1e-06
BLOCK = 128
STEP = 256
VMEM = 56 * 1024 * 1024


def mm(a, b):
    return jnp.dot(a, b, preferred_element_type=F32)


def mm_nt(a, b):
    return lax.dot_general(a, b, (((1,), (1,)), ((), ())), preferred_element_type=F32)


def mm_tn(a, b):
    return lax.dot_general(a, b, (((0,), (0,)), ((), ())), preferred_element_type=F32)


def ln_stats(v):
    centre = v - jnp.mean(v, -1, keepdims=True)
    rstd = lax.rsqrt(jnp.mean(centre * centre, -1, keepdims=True) + norm_eps)
    return centre * rstd, rstd


def ln_back(dy, vhat, rstd, gain):
    dhat = dy * gain
    return (dhat - jnp.mean(dhat, -1, keepdims=True) - vhat * jnp.mean(dhat * vhat, -1, keepdims=True)) * rstd


def gelu_pair(v):
    cdf = 0.5 * (1.0 + lax.erf(v * (1.0 / math.sqrt(2.0))))
    pdf = jnp.exp(-0.5 * v * v) * (1.0 / math.sqrt(2.0 * math.pi))
    return v * cdf, cdf + v * pdf


def colsum(v):
    return jnp.sum(v.astype(F32), 0)


def rowsum(v):
    return jnp.sum(v.astype(F32), 0, keepdims=True)


SMEM = pl.BlockSpec(memory_space=pltpu.SMEM)
ANY = pl.BlockSpec(memory_space=pl.ANY)


def whole(a):
    return pl.BlockSpec(a.shape, lambda i: (0,) * len(a.shape))


def shape(dims, dtype):
    return jax.ShapeDtypeStruct(dims, dtype)


def layer_of(a, level, rows=None, cols=None, at=lambda i: (0, 0)):
    rows, cols = rows or a.shape[1], cols or a.shape[2]
    return a, pl.BlockSpec((None, rows, cols), lambda i: (level, *at(i)))


def kernel_call(body, name, grid, ins, outs, flops, scratch=(), aliases=None):
    size = sum(a.size * a.dtype.itemsize for a, _ in ins) + sum(
        math.prod(s.shape) * s.dtype.itemsize for s, _ in outs
    )
    return pl.pallas_call(
        body,
        grid=grid,
        in_specs=[s for _, s in ins],
        out_specs=[s for _, s in outs],
        out_shape=[s for s, _ in outs],
        scratch_shapes=list(scratch),
        input_output_aliases=aliases or {},
        compiler_params=pltpu.CompilerParams(vmem_limit_bytes=VMEM),
        cost_estimate=pl.CostEstimate(flops=int(flops), bytes_accessed=int(size), transcendentals=0),
        name=name,
    )(*[a for a, _ in ins])


def routes(n):
    top, y = n >> 1, 2
    rest = [1 << k for k in range(2, n.bit_length() - 2)]
    for k in range(1, len(rest)):
        rest[k] |= rest[k - 1]
    halved = [(1, 1), (top, y), (y, top)]
    added = list(zip(rest, rest[::-1]))
    return halved, added


def swap(value, n, hop):
    return lax.ppermute(value, AXES, [(i, i ^ (hop[1] if i & 1 else hop[0])) for i in range(n)])


def device_index():
    return lax.axis_index("stream") * lax.axis_size("dp") + lax.axis_index("dp")


def my_bits(n):
    index = device_index()
    core = index % 2
    return [jnp.where(core == 0, (index // a) % 2, (index // b) % 2) for a, b in routes(n)[0]]


def sum_steps(bucket, n, bits):
    halved, added = routes(n)
    rows = bucket.shape[1]
    cur = bucket.reshape(2 * rows, -1)
    for hop, bit in zip(halved, bits):
        half = cur.shape[0] // 2
        theirs = lax.dynamic_slice_in_dim(cur, (1 - bit) * half, half, 0)
        mine = lax.dynamic_slice_in_dim(cur, bit * half, half, 0)
        got = yield theirs, hop
        cur = (mine.astype(F32) + got.astype(F32)).astype(BF)
    for hop in added:
        got = yield cur, hop
        cur = (cur.astype(F32) + got.astype(F32)).astype(BF)
    for hop, bit in reversed(list(zip(halved, bits))[1:]):
        got = yield cur, hop
        low = jnp.where(bit == 0, cur, got)
        high = jnp.where(bit == 0, got, cur)
        cur = jnp.concatenate([low, high], 0)
    got = yield cur, halved[0]
    return cur, got


class Lane:
    def __init__(self, bucket, n, bits):
        self.n, self.steps, self.result = n, sum_steps(bucket, n, bits), None
        self.ask = next(self.steps)

    def feed(self, got):
        try:
            self.ask = self.steps.send(got)
        except StopIteration as end:
            self.result = end.value


def stage(lanes, work=None, args=()):
    lanes = [lane for lane in lanes if lane.result is None]
    asked, args = lax.optimization_barrier(([lane.ask[0] for lane in lanes], args))
    got = [swap(value, lane.n, lane.ask[1]) for value, lane in zip(asked, lanes)]
    out = work(*args) if work else ()
    got, out = lax.optimization_barrier((got, out))
    for lane, value in zip(lanes, got):
        lane.feed(value)
    return out


def gather_rows(rows, n):
    index = device_index()
    cur = rows[None]
    order = [1 << k for k in range(1, n.bit_length() - 1)] + [1]
    for flip in order:
        got = swap(cur, n, (flip, flip))
        bit = (index // flip) % 2
        low = jnp.where(bit == 0, cur, got)
        high = jnp.where(bit == 0, got, cur)
        cur = jnp.stack([low, high], 1).reshape((2 * cur.shape[0],) + cur.shape[1:])
    k = len(order)
    cur = cur.reshape((2,) * k + rows.shape)
    places = [f.bit_length() - 1 for f in order]
    perm = [places.index(b) for b in reversed(range(k))]
    cur = cur.transpose(perm + [k, k + 1])
    return cur.reshape(n * rows.shape[0], rows.shape[1])


def halves(v, first):
    zero = jnp.zeros_like(v)
    return jnp.concatenate([jnp.where(first, v, zero), jnp.where(first, zero, v)], 0)


def join_halves(v, first):
    return jnp.where(first, v[: v.shape[0] // 2], v[v.shape[0] // 2 :])


def first_head(width):
    return lax.broadcasted_iota(jnp.int32, (1, 2 * width // HEADS), 1) < width // HEADS


def key_bias(lens_ref, block, span_short, count_short):
    key = lax.broadcasted_iota(jnp.int32, (BLOCK, 1), 0)
    query = lax.broadcasted_iota(jnp.int32, (1, BLOCK), 1)
    per = BLOCK // span_short
    blocks_short = count_short // per
    is_short = block < blocks_short
    at = jnp.where(is_short, block * per, count_short + block - blocks_short)
    limit = jnp.zeros((BLOCK, 1), jnp.int32)
    for s in range(per):
        inside = key // span_short == s
        limit = jnp.where(inside, jnp.where(is_short, lens_ref[at + jnp.where(is_short, s, 0)] + s * span_short, 0), limit)
    limit = jnp.where(is_short, limit, lens_ref[at])
    same = (key // span_short == query // span_short) | jnp.logical_not(is_short)
    return jnp.where((key < limit) & same, 0.0, -jnp.inf).astype(F32)


def vectors(level, width, bqv_ref, bresid_ref, gain_ref, shift_ref):
    row = slice(level, level + 1)
    low, high = slice(0, width), slice(width, 2 * width)
    return [ref[row, part] for ref in (bqv_ref, bresid_ref, gain_ref, shift_ref) for part in (low, high)]


def forward_body(
    span, count, lens_ref, short_ref, long_ref, wqkv_ref, wout_ref, win_ref, wback_ref, bin_ref, bqv_ref, bresid_ref, gain_ref, shift_ref,
    y_ref, qkv_ref, prob_ref, ctx_ref, hat1_ref, rstd1_ref, low_ref, act_ref, slope_ref, hat2_ref, rstd2_ref,
):
    step = pl.program_id(0)
    x = jnp.where(step == 0, short_ref[...], long_ref[...])
    rows, width = x.shape
    bq, bv, bo, bb, g1, g2, c1, c2 = vectors(0, width, bqv_ref, bresid_ref, gain_ref, shift_ref)
    pair = 2 * width // HEADS
    first = first_head(width)
    scale = 1.0 / math.sqrt(width // HEADS)
    bias = jnp.concatenate([bq, jnp.zeros_like(bq), bv], 1)
    qkv = (mm(x, wqkv_ref[...]) + bias).astype(BF)
    qkv_ref[...] = qkv
    blocks = []
    for b in range(rows // BLOCK):
        r = slice(b * BLOCK, (b + 1) * BLOCK)
        hide = key_bias(lens_ref, step * (rows // BLOCK) + b, span, count)
        hide = jnp.concatenate([hide, hide], 1)
        cols = []
        for p in range(HEADS // 2):
            q, k, v = (qkv[r, m * width + p * pair : m * width + (p + 1) * pair] for m in range(3))
            logit = mm_nt(k, halves(q, first)) * scale + hide
            power = jnp.exp(logit - jnp.max(logit, 0, keepdims=True))
            prob = (power * (1.0 / jnp.sum(power, 0, keepdims=True))).astype(BF)
            prob_ref[b, p] = prob
            cols.append(join_halves(mm_tn(prob, v), first))
        blocks.append(jnp.concatenate(cols, 1).astype(BF))
    ctx = jnp.concatenate(blocks, 0)
    ctx_ref[...] = ctx
    hat1, rstd1 = ln_stats(x.astype(F32) + mm(ctx, wout_ref[...]) + bo)
    normed = hat1 * g1 + c1
    low = normed.astype(BF)
    hat1_ref[...] = hat1.astype(BF)
    rstd1_ref[...] = jnp.broadcast_to(rstd1, rstd1_ref.shape)
    low_ref[...] = low
    act, slope = gelu_pair(mm(low, win_ref[...]) + bin_ref[0:1])
    act = act.astype(BF)
    act_ref[...] = act
    slope_ref[...] = slope.astype(BF)
    hat2, rstd2 = ln_stats(normed + mm(act, wback_ref[...]) + bb)
    hat2_ref[...] = hat2.astype(BF)
    rstd2_ref[...] = jnp.broadcast_to(rstd2, rstd2_ref.shape)
    y_ref[...] = (hat2 * g2 + c2).astype(BF)


def by_rows(cols):
    return pl.BlockSpec((STEP, cols), lambda i: (i, 0))


def from_buckets(short, long):
    width = short.shape[1]
    return [
        (short, pl.BlockSpec((STEP, width), lambda i: (0, 0))),
        (long, pl.BlockSpec((STEP, width), lambda i: (jnp.maximum(i - 1, 0), 0))),
    ]


def small_ins(w):
    return [(w[k], whole(w[k])) for k in ("b_qv", "b_resid", "gain", "shift")]


def forward(short, long, lens, w, span, count):
    rows, width = short.shape[0] + long.shape[0], short.shape[1]
    ff = w["in"].shape[2]
    per = STEP // BLOCK
    prob = pl.BlockSpec((per, HEADS // 2, BLOCK, 2 * BLOCK), lambda i: (i, 0, 0, 0))
    ins = [(lens, SMEM)] + from_buckets(short, long)
    ins += [layer_of(w[name], 0) for name in ("qkv", "out", "in", "back")] + [(w["b_in"], whole(w["b_in"]))] + small_ins(w)
    cols = [(width, BF), (3 * width, BF), None, (width, BF), (width, BF), (128, F32), (width, BF), (ff, BF), (ff, BF), (width, BF), (128, F32)]
    outs = [(shape((rows, c[0]), c[1]), by_rows(c[0])) if c else (shape((rows // BLOCK, HEADS // 2, BLOCK, 2 * BLOCK), BF), prob) for c in cols]
    body = functools.partial(forward_body, span, count)
    return kernel_call(body, "layer0_forward", (rows // STEP,), ins, outs, 2 * rows * width * (4 * width + 2 * ff))


def starts(sents, spans, rows):
    s = lax.broadcasted_iota(jnp.int32, (sents, rows), 0)
    r = lax.broadcasted_iota(jnp.int32, (sents, rows), 1)
    half = sents // 2
    at = jnp.where(s < half, s * spans[0], half * spans[0] + (s - half) * spans[1])
    return (r == at).astype(BF)


def spread(sents):
    a = lax.broadcasted_iota(jnp.int32, (sents * HEADS, sents), 0) // HEADS
    return (a == lax.broadcasted_iota(jnp.int32, (sents * HEADS, sents), 1)).astype(BF)


def own_head(sents, width):
    a = lax.broadcasted_iota(jnp.int32, (sents * HEADS, width), 0) % HEADS
    return a == lax.broadcasted_iota(jnp.int32, (sents * HEADS, width), 1) // (width // HEADS)


def sum_heads(v, keep, sents):
    return jnp.sum(jnp.where(keep, v, 0.0).reshape(sents, HEADS, v.shape[1]), 1)


def ask_body(spans, y_ref, lens_ref, wqkv_ref, bqv_ref, out_ref, wide_ref, key_ref, prob_ref, mixed_ref):
    y = y_ref[...]
    rows, width = y.shape
    sents = out_ref.shape[0]
    keep = own_head(sents, width)
    cls = mm(starts(sents, spans, rows), y).astype(BF)
    q = (mm(cls, wqkv_ref[:, :width]) + bqv_ref[1:2, :width]).astype(BF)
    wide = jnp.where(keep, mm(spread(sents), q), 0.0).astype(BF)
    key = mm_nt(wide, wqkv_ref[:, width : 2 * width]).astype(BF)
    half = sents // 2
    sent = lax.broadcasted_iota(jnp.int32, (sents * HEADS, 1), 0) // HEADS
    begin = jnp.where(sent < half, sent * spans[0], half * spans[0] + (sent - half) * spans[1])
    place = lax.broadcasted_iota(jnp.int32, (sents * HEADS, rows), 1) - begin
    seen = (place >= 0) & (place < lens_ref[...])
    logit = jnp.where(seen, mm_nt(key, y) * (1.0 / math.sqrt(width // HEADS)), -jnp.inf)
    power = jnp.exp(logit - jnp.max(logit, 1, keepdims=True))
    prob = (power * (1.0 / jnp.sum(power, 1, keepdims=True))).astype(BF)
    mixed = mm(prob, y).astype(BF)
    picked = sum_heads(mm(mixed, wqkv_ref[:, 2 * width :]), keep, sents)
    out_ref[:, :width] = (picked + bqv_ref[1:2, width:]).astype(BF)
    out_ref[:, width:] = cls
    wide_ref[...] = wide
    key_ref[...] = key
    prob_ref[...] = prob
    mixed_ref[...] = mixed


def ask(y, lens, w, spans, sents):
    rows, width = y.shape
    wide = sents * HEADS
    ins = [(y, whole(y)), (lens, whole(lens)), layer_of(w["qkv"], 1), (w["b_qv"], whole(w["b_qv"]))]
    outs = [(s, whole(s)) for s in (shape((sents, 2 * width), BF), shape((wide, width), BF), shape((wide, width), BF), shape((wide, rows), BF), shape((wide, width), BF))]
    return kernel_call(functools.partial(ask_body, spans), "layer1_ask", (1,), ins, outs, 2 * wide * width * (2 * rows + 3 * width))


def top_forward(ctx, cls, wout_ref, win_ref, bin_ref, bo, g1, c1):
    hat1, rstd1 = ln_stats(cls.astype(F32) + mm(ctx, wout_ref[...]) + bo)
    normed = hat1 * g1 + c1
    low = normed.astype(BF)
    return hat1, rstd1, normed, low, mm(low, win_ref[...]) + bin_ref[1:2]


def gelu(v):
    return v * (0.5 * (1.0 + lax.erf(v * (1.0 / math.sqrt(2.0)))))


def top_body(index_ref, every_ref, pair_ref, wout_ref, win_ref, wback_ref, bin_ref, bqv_ref, bresid_ref, gain_ref, shift_ref,
             datt_ref, dctx_ref, dy_ref, hid_s, hat1_s, rstd1_s, hat2_s, rstd2_s):
    width = dy_ref.shape[1]
    pairs = pair_ref.shape[0]
    sents = datt_ref.shape[0]
    _, _, bo, bb, g1, g2, c1, c2 = vectors(1, width, bqv_ref, bresid_ref, gain_ref, shift_ref)
    hat1, rstd1, normed, low, hid = top_forward(every_ref[:, :width], every_ref[:, width:], wout_ref, win_ref, bin_ref, bo, g1, c1)
    hid_s[...] = hid
    hat1_s[...] = hat1
    rstd1_s[...] = jnp.broadcast_to(rstd1, rstd1_s.shape)
    hat2, rstd2 = ln_stats(normed + mm(gelu(hid).astype(BF), wback_ref[...]) + bb)
    hat2_s[...] = hat2
    rstd2_s[...] = jnp.broadcast_to(rstd2, rstd2_s.shape)
    pooled = hat2 * g2 + c2
    radius = lax.rsqrt(jnp.sum(pooled * pooled, -1, keepdims=True) + unit_eps)
    unit = pooled * radius
    src, tgt = unit[:pairs].astype(BF), unit[pairs:].astype(BF)
    positive = (pair_ref[...] == lax.broadcasted_iota(jnp.int32, (pairs, pairs), 1)).astype(F32)
    logits = logit_scale * (mm_nt(src, tgt) - margin * positive)

    def soft(axis):
        powers = jnp.exp(logits - jnp.max(logits, axis, keepdims=True))
        return powers / jnp.sum(powers, axis, keepdims=True)

    dscore = (0.5 * logit_scale * (soft(1) + soft(0) - 2.0 * positive)).astype(BF)
    dunit = jnp.concatenate([mm(dscore, tgt), mm_tn(dscore, src)], 0)
    dy_ref[...] = radius * (dunit - unit * jnp.sum(dunit * unit, -1, keepdims=True))
    mine = pl.ds(pl.multiple_of(index_ref[0] * sents, sents), sents)
    dmixed = ln_back(dy_ref[mine], hat2_s[mine], rstd2_s[mine, 0:1], g2)
    dhidden = (mm_nt(dmixed.astype(BF), wback_ref[...]) * gelu_pair(hid_s[mine])[1]).astype(BF)
    dnormed = dmixed + mm_nt(dhidden, win_ref[...])
    datt = ln_back(dnormed, hat1_s[mine], rstd1_s[mine, 0:1], g1)
    datt_ref[...] = datt
    dctx_ref[...] = mm_nt(datt.astype(BF), wout_ref[...]).astype(BF)


def top_ins(w):
    return [layer_of(w[k], 1) for k in ("out", "in", "back")] + [(w["b_in"], whole(w["b_in"]))] + small_ins(w)


def top(index, every, pair, w, sents):
    rows, width = every.shape[0], every.shape[1] // 2
    ff = w["in"].shape[2]
    ins = [(index, SMEM), (every, whole(every)), (pair, whole(pair))] + top_ins(w)
    outs = [(s, whole(s)) for s in (shape((sents, width), F32), shape((sents, width), BF), shape((rows, width), F32))]
    scratch = [pltpu.VMEM((rows, c), F32) for c in (ff, width, 128, width, 128)]
    return kernel_call(top_body, "top", (1,), ins, outs, 2 * rows * width * (width + 2 * ff), scratch)


def top_grads_body(every_ref, dy_ref, wout_ref, win_ref, wback_ref, bin_ref, bqv_ref, bresid_ref, gain_ref, shift_ref,
                   gout_ref, gin_ref, gback_ref, sums_ref, sumin_ref):
    width = dy_ref.shape[1]
    _, _, bo, bb, g1, g2, c1, c2 = vectors(1, width, bqv_ref, bresid_ref, gain_ref, shift_ref)
    ctx = every_ref[:, :width]
    hat1, rstd1, normed, low, hid = top_forward(ctx, every_ref[:, width:], wout_ref, win_ref, bin_ref, bo, g1, c1)
    act, slope = gelu_pair(hid)
    act = act.astype(BF)
    hat2, rstd2 = ln_stats(normed + mm(act, wback_ref[...]) + bb)
    dy = dy_ref[...]
    dmixed = ln_back(dy, hat2, rstd2, g2)
    dmixed_low = dmixed.astype(BF)
    gback_ref[...] = mm_tn(act, dmixed_low)
    dhidden = (mm_nt(dmixed_low, wback_ref[...]) * slope).astype(BF)
    gin_ref[...] = mm_tn(low, dhidden)
    dnormed = dmixed + mm_nt(dhidden, win_ref[...])
    datt = ln_back(dnormed, hat1, rstd1, g1)
    datt_low = datt.astype(BF)
    gout_ref[...] = mm_tn(ctx, datt_low)
    sumin_ref[...] = rowsum(dhidden)
    parts = (datt, dmixed, dnormed * hat1, dy * hat2, dnormed, dy, mm_nt(datt_low, wout_ref[...]).astype(BF))
    for k, part in enumerate(parts):
        sums_ref[k : k + 1] = rowsum(part)
    sums_ref[7:8] = jnp.zeros((1, width), F32)


def top_grads(every, dy, w):
    width = dy.shape[1]
    ff = w["in"].shape[2]
    rows = every.shape[0]
    ins = [(every, whole(every)), (dy, whole(dy))] + top_ins(w)

    def upper(a, b):
        return shape((2, a, b), F32), pl.BlockSpec((None, a, b), lambda i: (1, 0, 0))

    sums, sumin = shape((8, width), F32), shape((1, ff), F32)
    outs = [upper(width, width), upper(width, ff), upper(ff, width), (sums, whole(sums)), (sumin, whole(sumin))]
    return kernel_call(top_grads_body, "top_grads", (1,), ins, outs, 6 * rows * width * (width + 2 * ff))


def ask_back_body(spans, y_ref, wide_ref, key_ref, prob_ref, mixed_ref, wqkv_ref, dctx_ref, datt_ref,
                  hat2_ref, rstd2_ref, gain_ref, act_ref, bucket_ref, dmixed_ref, low_ref, sums_ref):
    step = pl.program_id(0)
    rows, width = y_ref.shape
    ff = pl.num_programs(0) * width

    @pl.when(step == 0)
    def _():
        y = y_ref[...]
        sents = dctx_ref.shape[0]
        keep = own_head(sents, width)
        first = starts(sents, spans, rows)
        prob_low = prob_ref[...]
        wide = wide_ref[...]
        d_wide = jnp.where(keep, mm(spread(sents), dctx_ref[...]), 0.0).astype(BF)
        d_value = mm_nt(d_wide, wqkv_ref[:, 2 * width :]).astype(BF)
        dprob = mm_nt(d_value, y)
        prob = prob_low.astype(F32)
        dlogit = prob * (dprob - jnp.sum(prob * dprob, 1, keepdims=True))
        dscore = (dlogit * (1.0 / math.sqrt(width // HEADS))).astype(BF)
        pulled = mm(dscore, y).astype(BF)
        dq = sum_heads(mm(pulled, wqkv_ref[:, width : 2 * width]), keep, sents).astype(BF)
        dcls = mm_nt(dq, wqkv_ref[:, :width]) + datt_ref[...]
        high = dcls.astype(BF)
        left = jnp.concatenate([dscore, prob_low, first, first], 0)
        right = jnp.concatenate([key_ref[...], d_value, high, (dcls - high.astype(F32)).astype(BF)], 0)
        dy = mm_tn(left, right)
        hat2 = hat2_ref[...].astype(F32)
        dmixed = ln_back(dy, hat2, rstd2_ref[:, 0:1], gain_ref[0:1, width:])
        low_ref[...] = dmixed.astype(BF)
        dmixed_ref[...] = dmixed
        cls = mm(first, y).astype(BF)
        bucket_ref[ff : ff + width] = mm_tn(cls, dq).astype(BF)
        bucket_ref[ff + width : ff + 2 * width] = mm_tn(pulled, wide).astype(BF)
        bucket_ref[ff + 2 * width :] = mm_tn(mixed_ref[...], d_wide).astype(BF)
        sums_ref[0:1] = rowsum(dmixed)
        sums_ref[1:2] = rowsum(dy * hat2)
        sums_ref[2:3] = rowsum(dy)
        sums_ref[3:4] = rowsum(dq)
        sums_ref[4:8] = jnp.zeros((4, width), F32)

    bucket_ref[pl.ds(pl.multiple_of(step * width, width), width)] = mm_tn(act_ref[...], low_ref[...]).astype(BF)


def ask_back(y, kept, w, dctx, datt, hat2, rstd2, act, spans):
    rows, width = y.shape
    ff = act.shape[1]
    ins = [(a, whole(a)) for a in (y, *kept)] + [layer_of(w["qkv"], 1)]
    ins += [(a, whole(a)) for a in (dctx, datt, hat2, rstd2, w["gain"])] + [(act, pl.BlockSpec((rows, width), lambda i: (0, i)))]
    outs = [(s, whole(s)) for s in (shape((ff + 3 * width, width), BF), shape((rows, width), F32), shape((rows, width), BF), shape((8, width), F32))]
    return kernel_call(functools.partial(ask_back_body, spans), "layer1_ask_back", (ff // width,), ins, outs, 2 * rows * width * ff + 2 * rows * width * 512)


VECTOR_ROWS = 64


def hidden_back_body(low_ref, slope_ref, wback_ref, nlow_ref, bucket_ref, dhidden_ref, sumin_ref):
    dhidden = (mm_nt(low_ref[...], wback_ref[...]) * slope_ref[...].astype(F32)).astype(BF)
    dhidden_ref[...] = dhidden
    bucket_ref[...] = mm_tn(nlow_ref[...], dhidden).astype(BF)
    sumin_ref[0] = rowsum(dhidden)


def hidden_back(low, slope, nlow, w):
    rows, width = low.shape
    ff = slope.shape[1]
    cols = pl.BlockSpec((rows, width), lambda i: (0, i))
    ins = [(low, whole(low)), (slope, cols), layer_of(w["back"], 0, width, width, lambda i: (i, 0)), (nlow, whole(nlow))]
    outs = [(shape((2, ff + VECTOR_ROWS, width), BF), pl.BlockSpec((None, width, width), lambda i: (0, i, 0)))]
    outs += [(shape((rows, ff), BF), cols), (shape((ff // width, 1, width), F32), pl.BlockSpec((1, 1, width), lambda i: (i, 0, 0)))]
    return kernel_call(hidden_back_body, "layer0_hidden_back", (ff // width,), ins, outs, 4 * rows * width * ff)


def normed_back_body(dhidden_ref, dmixed_ref, win_ref, hat1_ref, rstd1_ref, gain_ref, ctx_ref, wout_ref, _, bucket_ref, datt_ref, dctx_ref, sums_ref, acc):
    step = pl.program_id(0)
    width = dmixed_ref.shape[1]

    @pl.when(step == 0)
    def _():
        acc[...] = jnp.zeros_like(acc)
        sums_ref[...] = jnp.zeros_like(sums_ref)

    dnormed = dmixed_ref[...] + mm_nt(dhidden_ref[...], win_ref[...])
    hat1 = hat1_ref[...].astype(F32)
    datt = ln_back(dnormed, hat1, rstd1_ref[:, 0:1], gain_ref[0:1, :width])
    low = datt.astype(BF)
    datt_ref[...] = datt
    dctx_ref[...] = mm_nt(low, wout_ref[...]).astype(BF)
    acc[...] += mm_tn(ctx_ref[...], low)
    sums_ref[0:1] += rowsum(datt)
    sums_ref[1:2] += rowsum(dnormed * hat1)
    sums_ref[2:3] += rowsum(dnormed)

    @pl.when(step == pl.num_programs(0) - 1)
    def _():
        bucket_ref[...] = acc[...].astype(BF)


def normed_back(dhidden, dmixed, hat1, rstd1, ctx, bucket, w):
    rows, width = dmixed.shape
    ff = dhidden.shape[1]
    ins = [(dhidden, by_rows(ff)), (dmixed, by_rows(width)), layer_of(w["in"], 0), (hat1, by_rows(width)), (rstd1, by_rows(128)), (w["gain"], whole(w["gain"]))]
    ins += [(ctx, by_rows(width)), layer_of(w["out"], 0), (bucket, ANY)]
    sums = shape((8, width), F32)
    outs = [(shape(bucket.shape, BF), pl.BlockSpec((None, width, width), lambda i: (1, 0, 0)))]
    outs += [(shape((rows, width), F32), by_rows(width)), (shape((rows, width), BF), by_rows(width)), (sums, whole(sums))]
    return kernel_call(normed_back_body, "layer0_normed_back", (rows // STEP,), ins, outs, 2 * rows * width * (ff + 2 * width), [pltpu.VMEM((width, width), F32)], {8: 0})


def attention_back_body(qkv_ref, prob_ref, dctx_ref, short_ref, long_ref, sums1_ref, sums2_ref, sumin_ref, _, dqkv_ref, bucket_ref, acc, sums, thirds, vec, done):
    step = pl.program_id(0)
    x = jnp.where(step == 0, short_ref[...], long_ref[...])
    rows, width = x.shape
    pair = 2 * width // HEADS
    first = first_head(width)
    scale = 1.0 / math.sqrt(width // HEADS)

    @pl.when(step == 0)
    def _():
        acc[...] = jnp.zeros_like(acc)
        sums[...] = jnp.zeros_like(sums)

    for b in range(rows // BLOCK):
        r = slice(b * BLOCK, (b + 1) * BLOCK)
        for p in range(HEADS // 2):
            c = [slice(m * width + p * pair, m * width + (p + 1) * pair) for m in range(3)]
            q, k, v = (qkv_ref[r, s] for s in c)
            dd = halves(dctx_ref[r, c[0]], first)
            low = prob_ref[b, p]
            prob = low.astype(F32)
            dprob = mm_nt(v, dd)
            dlogit = prob * (dprob - jnp.sum(prob * dprob, 0, keepdims=True))
            dscore = (dlogit * scale).astype(BF)
            dqkv_ref[r, c[0]] = join_halves(mm_tn(dscore, k), first).astype(BF)
            dqkv_ref[r, c[1]] = mm(dscore, halves(q, first)).astype(BF)
            dqkv_ref[r, c[2]] = mm(low, dd).astype(BF)
    dqkv = dqkv_ref[...]
    acc[...] += mm_tn(x, dqkv)
    sums[0:1] += rowsum(dqkv)

    @pl.when(step == pl.num_programs(0) - 1)
    def _():
        for m in range(3):
            thirds[m * width : (m + 1) * width] = acc[:, m * width : (m + 1) * width].astype(BF)
        rows_of = [sums[0:1, :width], sums[0:1, 2 * width :]]
        for k in range(3):
            rows_of += [sums1_ref[k : k + 1], sums2_ref[k : k + 1]]
        rows_of += [sumin_ref[k] for k in range(sumin_ref.shape[0])]
        rows_of += [sums2_ref[3:4], jnp.zeros((3, width), F32)]
        vec[...] = jnp.zeros_like(vec)
        vec[0:16] = jnp.concatenate(rows_of, 0).astype(BF)
        size = bucket_ref.shape[1]
        copies = [
            pltpu.make_async_copy(thirds, bucket_ref.at[1, width : 4 * width], done.at[0]),
            pltpu.make_async_copy(vec, bucket_ref.at[0, size - VECTOR_ROWS : size], done.at[1]),
        ]
        for copy in copies:
            copy.start()
        for copy in copies:
            copy.wait()


def attention_back(qkv, prob, dctx, sums1, bucket, sums2, sumin, short, long):
    rows, width = dctx.shape
    per = STEP // BLOCK
    ins = [(qkv, by_rows(3 * width)), (prob, pl.BlockSpec((per,) + prob.shape[1:], lambda i: (i, 0, 0, 0))), (dctx, by_rows(width))]
    ins += from_buckets(short, long) + [(a, whole(a)) for a in (sums1, sums2, sumin)]
    ins += [(bucket, ANY)]
    outs = [(shape((rows, 3 * width), BF), by_rows(3 * width)), (shape(bucket.shape, BF), ANY)]
    scratch = [pltpu.VMEM((width, 3 * width), F32), pltpu.VMEM((8, 3 * width), F32)]
    scratch += [pltpu.VMEM((3 * width, width), BF), pltpu.VMEM((VECTOR_ROWS, width), BF), pltpu.SemaphoreType.DMA((2,))]
    flops = 2 * rows * width * (3 * width + 10 * BLOCK)
    return kernel_call(attention_back_body, "layer0_attention_back", (rows // STEP,), ins, outs, flops, scratch, {8: 1})


def input_back_body(dqkv_ref, datt_ref, wqkv_ref, short_ref, long_ref):
    dx = datt_ref[...] + mm_nt(dqkv_ref[...], wqkv_ref[...])

    @pl.when(pl.program_id(0) == 0)
    def _():
        short_ref[...] = dx

    @pl.when(pl.program_id(0) > 0)
    def _():
        long_ref[...] = dx


def input_back(dqkv, datt, w, cut):
    rows, width = datt.shape
    ins = [(dqkv, by_rows(3 * width)), (datt, by_rows(width)), layer_of(w["qkv"], 0)]
    outs = [
        (shape((cut, width), F32), pl.BlockSpec((STEP, width), lambda i: (0, 0))),
        (shape((rows - cut, width), F32), pl.BlockSpec((STEP, width), lambda i: (jnp.maximum(i - 1, 0), 0))),
    ]
    return kernel_call(input_back_body, "layer0_input_back", (rows // STEP,), ins, outs, 2 * rows * width * 3 * width)


def unpack_call(body, name, bit, grid, ins, outs, aliases, size):
    return pl.pallas_call(
        body,
        grid_spec=pltpu.PrefetchScalarGridSpec(
            num_scalar_prefetch=1,
            grid=grid,
            in_specs=[s for _, s in ins],
            out_specs=[s for _, s in outs],
        ),
        out_shape=[s for s, _ in outs],
        input_output_aliases=aliases,
        compiler_params=pltpu.CompilerParams(vmem_limit_bytes=VMEM),
        cost_estimate=pl.CostEstimate(flops=0, bytes_accessed=size, transcendentals=0),
        name=name,
    )(bit, *[a for a, _ in ins])


def in_order(bit_ref, mine_ref, theirs_ref):
    mine, theirs = mine_ref[...].astype(F32), theirs_ref[...].astype(F32)
    low = bit_ref[0] == 0
    return jnp.where(low, mine, theirs), jnp.where(low, theirs, mine)


def unpack_first(bit, pair, back):
    _, ff, width = back.shape
    rows = width // 2
    steps = pair[0].shape[0] // rows
    block = pl.BlockSpec((rows, width), lambda j, bit: (j, 0))

    def at_qkv(j, bit):
        j = jnp.maximum(j - 1, 0)
        return 1, j % 2, j // 2

    def body(bit_ref, mine_ref, theirs_ref, _, qkv_ref, back_ref):
        step = pl.program_id(0)
        low, high = in_order(bit_ref, mine_ref, theirs_ref)
        back_ref[pl.ds(pl.multiple_of(step * rows, rows), rows)] = low

        @pl.when(step == 0)
        def _():
            back_ref[steps * rows :] = high

        @pl.when(step > 0)
        def _():
            qkv_ref[...] = high

    outs = [
        (shape((2, width, 3 * width), F32), pl.BlockSpec((None, rows, width), at_qkv)),
        (shape(back.shape, F32), pl.BlockSpec((None, ff, width), lambda j, bit: (0, 0, 0))),
    ]
    ins = [(pair[0], block), (pair[1], block), (back, ANY)]
    return unpack_call(body, "unpack_first", bit, (steps,), ins, outs, {3: 1}, 12 * steps * rows * width)


def unpack_second(bit, pair, gin, gout, qkv, sums, sumin):
    _, width, ff = gin.shape
    steps = ff // width
    block = pl.BlockSpec((width, width), lambda j, bit: (j, 0))
    tail = pl.BlockSpec((VECTOR_ROWS, width), lambda j, bit: (ff // VECTOR_ROWS, 0))

    def fixed(a):
        return pl.BlockSpec(a.shape, lambda j, bit: (0,) * len(a.shape))

    def body(bit_ref, mine_ref, theirs_ref, mine_v, theirs_v, sums_ref, sumin_ref, _, __, ___,
             in_ref, out_ref, qkv_ref, bqv_ref, bresid_ref, gain_ref, shift_ref, bin_ref):
        step = pl.program_id(0)
        low, high = in_order(bit_ref, mine_ref, theirs_ref)
        in_ref[...] = low

        @pl.when(step > 0)
        def _():
            qkv_ref[...] = high

        @pl.when(step == 0)
        def _():
            out_ref[...] = high
            value, _ = in_order(bit_ref, mine_v, theirs_v)
            for ref, lower, upper in (
                (bqv_ref, (value[0:1], value[1:2]), (value[12:13], sums_ref[6:7])),
                (bresid_ref, (value[2:3], value[3:4]), (sums_ref[0:1], sums_ref[1:2])),
                (gain_ref, (value[4:5], value[5:6]), (sums_ref[2:3], sums_ref[3:4])),
                (shift_ref, (value[6:7], value[7:8]), (sums_ref[4:5], sums_ref[5:6])),
            ):
                for level, both in enumerate((lower, upper)):
                    for k in range(2):
                        ref[level : level + 1, k * width : (k + 1) * width] = both[k]
            for k in range(ff // width):
                bin_ref[0:1, k * width : (k + 1) * width] = value[8 + k : 9 + k]
            bin_ref[1:2, :] = sumin_ref[...]

    outs = [
        (shape(gin.shape, F32), pl.BlockSpec((None, width, width), lambda j, bit: (0, 0, j))),
        (shape(gout.shape, F32), pl.BlockSpec((None, width, width), lambda j, bit: (0, 0, 0))),
        (shape(qkv.shape, F32), pl.BlockSpec((None, width, width), lambda j, bit: (0, 0, jnp.maximum(j - 1, 0)))),
    ]
    outs += [(s, fixed(s)) for s in [shape((2, 2 * width), F32)] * 4 + [shape((2, ff), F32)]]
    ins = [(pair[0], block), (pair[1], block), (pair[0], tail), (pair[1], tail), (sums, fixed(sums)), (sumin, fixed(sumin))]
    ins += [(gin, ANY), (gout, ANY), (qkv, ANY)]
    return unpack_call(body, "unpack_second", bit, (steps,), ins, outs, {7: 0, 8: 1, 9: 2}, 12 * steps * width * width)


def top_rows(context, resid, pair_index, weights):
    w_qkv, b_qv, w_out, b_resid, gain, shift, w_in, b_in, w_back = weights
    rows, width = context.shape
    pairs = rows // 2
    hat1, rstd1 = ln_stats(resid.astype(F32) + mm(context, w_out) + b_resid[:width])
    normed = hat1 * gain[:width] + shift[:width]
    normed_low = normed.astype(BF)
    activ, slope = gelu_pair(mm(normed_low, w_in) + b_in)
    activ = activ.astype(BF)
    hat2, rstd2 = ln_stats(normed + mm(activ, w_back) + b_resid[width:])
    pooled = hat2 * gain[width:] + shift[width:]
    radius = lax.rsqrt(jnp.sum(pooled * pooled, -1, keepdims=True) + unit_eps)
    unit = pooled * radius
    unit_low = unit.astype(BF)
    src, tgt = unit_low[:pairs], unit_low[pairs:]
    positive = (pair_index[:, None] == jnp.arange(pairs)[None, :]).astype(F32)
    logits = logit_scale * (mm_nt(src, tgt) - margin * positive)

    def soft(axis):
        powers = jnp.exp(logits - jnp.max(logits, axis, keepdims=True))
        return powers / jnp.sum(powers, axis, keepdims=True)

    dscore = (0.5 * logit_scale * (soft(1) + soft(0) - 2.0 * positive)).astype(BF)
    dunit = jnp.concatenate([mm(dscore, tgt), mm_tn(dscore, src)], 0)
    dy = radius * (dunit - unit * jnp.sum(dunit * unit, -1, keepdims=True))
    dg2, dc2 = colsum(dy * hat2), colsum(dy)
    dmixed = ln_back(dy, hat2, rstd2, gain[width:])
    dmixed_low = dmixed.astype(BF)
    dhidden = (mm_nt(dmixed_low, w_back) * slope).astype(BF)
    dnormed = dmixed + mm_nt(dhidden, w_in)
    dg1, dc1 = colsum(dnormed * hat1), colsum(dnormed)
    datt = ln_back(dnormed, hat1, rstd1, gain[:width])
    datt_low = datt.astype(BF)
    dctx = mm_nt(datt_low, w_out).astype(BF)
    grads = (mm_tn(context, datt_low), mm_tn(normed_low, dhidden), mm_tn(activ, dmixed_low))
    vectors = dict(
        bv=colsum(dctx),
        b_resid=jnp.concatenate([colsum(datt), colsum(dmixed)]),
        gain=jnp.concatenate([dg1, dg2]),
        shift=jnp.concatenate([dc1, dc2]),
        b_in=colsum(dhidden),
    )
    return datt, dctx, grads, vectors


def per_device(short_tokens, long_tokens, short_len, long_len, pair_index, *params):
    n = lax.axis_size("stream") * lax.axis_size("dp")
    index = lax.axis_index("stream") * lax.axis_size("dp") + lax.axis_index("dp")
    width = short_tokens.shape[-1]
    spans = (short_tokens.shape[2], long_tokens.shape[2])
    counts = (short_tokens.shape[1], long_tokens.shape[1])
    sents = sum(counts)
    w_qkv, b_qv, w_out, b_resid, gain, shift, w_in, b_in, w_back = params
    w = dict(qkv=w_qkv, b_qv=b_qv, out=w_out, b_resid=b_resid, gain=gain, shift=shift, b_in=b_in, back=w_back) | {"in": w_in}
    short, long = short_tokens.reshape(-1, width), long_tokens.reshape(-1, width)
    lens = jnp.concatenate([short_len.reshape(-1), long_len.reshape(-1)])
    lens_wide = jnp.repeat(lens, HEADS)[:, None]

    y, qkv, prob, ctx, hat1, rstd1, nlow, act, slope, hat2, rstd2 = forward(short, long, lens, w, spans[0], counts[0])
    sent, *kept = ask(y, lens_wide, w, spans, sents)
    every = gather_rows(sent, n)
    one_kernel = n * sents <= 512
    if one_kernel:
        own_datt, own_dctx, dy_top = top(index.reshape(1).astype(jnp.int32), every, pair_index[:, None], w, sents)
    else:
        datt, dctx, top_g, top_vec = top_rows(every[:, :width], every[:, width:], pair_index, tuple(p[1] for p in params))
        own_datt = lax.dynamic_slice_in_dim(datt, index * sents, sents, 0)
        own_dctx = lax.dynamic_slice_in_dim(dctx, index * sents, sents, 0)
    bits = my_bits(n)
    bit = bits[0].reshape(1).astype(jnp.int32)

    bucket1, dmixed, dmixed_low, sums2 = ask_back(y, kept, w, own_dctx, own_datt, hat2, rstd2, act, spans)
    first = Lane(bucket1.reshape(2, -1, width), n, bits)
    bucket2, dhidden, sumin = stage([first], lambda *a: hidden_back(*a, w), (dmixed_low, slope, nlow))
    bucket2, datt0, dctx0, sums1 = stage([first], lambda *a: normed_back(*a, w), (dhidden, dmixed, hat1, rstd1, ctx, bucket2))
    dqkv, bucket2 = stage([first], lambda *a: attention_back(*a, sums2, sumin, short, long), (qkv, prob, dctx0, sums1, bucket2))
    second = Lane(bucket2, n, bits)
    both = [first, second]
    dshort, dlong = stage(both, lambda *a: input_back(*a, w, counts[0] * spans[0]), (dqkv, datt0))
    if one_kernel:
        gout1, gin1, gback1, top_sums, top_sumin = stage(both, lambda *a: top_grads(*a, w), (every, dy_top))
    else:
        gout1, gin1, gback1 = (jnp.stack([g, g]) for g in top_g)
        rows_of = [top_vec[k].reshape(2, width) for k in ("b_resid", "gain", "shift")]
        top_sums = jnp.concatenate(rows_of + [top_vec["bv"][None], jnp.zeros((1, width), F32)], 0)
        top_sumin = top_vec["b_in"][None]
    while first.result is None:
        stage(both)
    g_qkv, g_back = stage([second], lambda *a: unpack_first(bit, *a), (first.result, gback1))
    while second.result is None:
        stage(both)
    g_in, g_out, g_qkv, g_bqv, g_bresid, g_gain, g_shift, g_bin = unpack_second(bit, second.result, gin1, gout1, g_qkv, top_sums, top_sumin)
    outs = (g_qkv, g_bqv, g_out, g_bresid, g_gain, g_shift, g_in, g_bin, g_back)
    return outs + (dshort.reshape((1, counts[0], spans[0], width)), dlong.reshape((1, counts[1], spans[1], width)))


def solution(mesh):
    split = P("stream", "dp", None, None)
    in_specs = (split, split, P("stream", "dp"), P("stream", "dp")) + (P(),) * 10
    out_specs = (P(),) * 9 + (split, split)
    return jax.shard_map(per_device, mesh=mesh, in_specs=in_specs, out_specs=out_specs, check_vma=False)
```

profile of v0, /device:TPU:0, one launch (start us, length us, event | category | flops | bytes accessed | tf_op | source)
XLA Modules:
  0.0 251.4 jit_solution(6056206273024339232)
XLA Ops:
  2.2 21.6 %layer0_forward.1 = (bf16[1280,512]{1,0:T(8,128)(2,1)}, bf16[1280,1536]{1,0:T(8,128)(2,1)}, bf16[10,4,128,256]{3,2,1,0:T(8,128)(2,1)}, bf16[1280,512]{1,0:T(8,12...) custom-call(s32[16]{0:T(128)} %copy-done.7, ...), custom_call_target="tpu_custom_call" | custom-call | flops 8053063680 | bytes 38846528 | tf_op jit(solution)/shard_map/layer0_forward/pallas_call | solution.py:82
  23.8 4.5 %layer1_ask.1 = (bf16[16,1024]{1,0:T(8,128)(2,1)}, bf16[128,512]{1,0:T(8,128)(2,1)}, bf16[128,512]{1,0:T(8,128)(2,1)}, bf16[128,1280]{1,0:T(8,128)(2,1)}, bf16[128,512]{1,0:T(8,128)(2,1)}) custom-call(bf16[1280,512]{1,0:T(8,128)(2,1)} %get-tuple-element.127.y_ref, s32[128,1]{1,0:T(8,128)} %broadcast_in_dim_reshape.4.lens_ref, ...), custom_call_target="tpu_custom_call" | custom-call | flops 536870912 | bytes 5218816 | tf_op jit(solution)/shard_map/layer1_ask/pallas_call | solution.py:82
  28.4 3.0 %collective-permute-start = (bf16[1,16,1024]{2,1,0:T(8,128)(2,1)}, bf16[1,16,1024]{2,1,0:T(8,128)(2,1)S(1)}, u32[]{:S(2)}, u32[]{:S(2)}) collective-permute-start(bf16[1,16,1024]{2,1,0:T(8,128)(2,1)} %bitcast.60), channel_id=1, source_target_pairs={{0,2},{1,3},{2,0},{3,1},{4,6},{5,7},{6,4},{7,5},{8,10},{9,11},{10,... | collective-permute-start | bytes 98312 | tf_op jit(solution)/shard_map/ppermute | solution.py:107
  31.3 2.1 collective-permute-done
  34.2 2.1 collective-permute-start.1
  36.4 2.2 collective-permute-done.1
  38.7 3.1 %collective-permute-start.2 = (bf16[4,16,1024]{2,1,0:T(8,128)(2,1)S(1)}, bf16[4,16,1024]{2,1,0:T(8,128)(2,1)S(1)}, u32[]{:S(2)}, u32[]{:S(2)}) collective-permute-start(bf16[4,16,1024]{2,1,0:T(8,128)(2,1)S(1)} %bitcast.59), channel_id=1, source_target_pairs={{0,8},{1,9},{2,10},{3,11},{4,12},{5,13},{6,14},{7,15},{8,0},{9,1},... | collective-permute-start | bytes 393224 | tf_op jit(solution)/shard_map/ppermute | solution.py:107
  41.8 3.0 %collective-permute-done.2 = bf16[4,16,1024]{2,1,0:T(8,128)(2,1)S(1)} collective-permute-done((bf16[4,16,1024]{2,1,0:T(8,128)(2,1)S(1)}, bf16[4,16,1024]{2,1,0:T(8,128)(2,1)S(1)}, u32[]{:S(2)}, u32[]{:S(2)}) %collective-permute-start.2) | collective-permute-done | bytes 131104 | tf_op jit(solution)/shard_map/ppermute | solution.py:107
  44.8 3.3 %collective-permute-start.3 = (bf16[8,16,1024]{2,1,0:T(8,128)(2,1)S(1)}, bf16[8,16,1024]{2,1,0:T(8,128)(2,1)S(1)}, u32[]{:S(2)}, u32[]{:S(2)}) collective-permute-start(bf16[8,16,1024]{2,1,0:T(8,128)(2,1)S(1)} %bitcast.58), channel_id=1, source_target_pairs={{0,16},{1,17},{2,18},{3,19},{4,20},{5,21},{6,22},{7,23},{8,24},{9,... | collective-permute-start | bytes 786440 | tf_op jit(solution)/shard_map/ppermute | solution.py:107
  48.1 4.4 %collective-permute-done.3 = bf16[8,16,1024]{2,1,0:T(8,128)(2,1)S(1)} collective-permute-done((bf16[8,16,1024]{2,1,0:T(8,128)(2,1)S(1)}, bf16[8,16,1024]{2,1,0:T(8,128)(2,1)S(1)}, u32[]{:S(2)}, u32[]{:S(2)}) %collective-permute-start.3) | collective-permute-done | bytes 262176 | tf_op jit(solution)/shard_map/ppermute | solution.py:107
  55.9 9.5 %top.1 = (f32[16,512]{1,0:T(8,128)}, bf16[16,512]{1,0:T(8,128)(2,1)}, f32[512,512]{1,0:T(8,128)}) custom-call(s32[1]{0:T(128)} %bitcast.5.index_ref, bf16[512,1024]{1,0:T(8,128)(2,1)} %bitcast.53, s32[256,1]{1,0:T(8,128)} %copy.49.pair_ref, bf16[2,512,512]{2,1,0:T(8,128)(2,1)} %wout_ref.7, bf16[2,512,2048]{2,1,0:T(8,128)(2,1)} %win_ref.7, ...), custom_call_target="tpu_custom_call" | custom-call | flops 2415919104 | bytes 11633668 | tf_op jit(solution)/shard_map/top/pallas_call | solution.py:82
  65.4 13.3 %layer1_ask_back.1 = (bf16[3584,512]{1,0:T(8,128)(2,1)}, f32[1280,512]{1,0:T(8,128)}, bf16[1280,512]{1,0:T(8,128)(2,1)}, f32[8,512]{1,0:T(8,128)}) custom-call(bf16[1280,512]{1,0:T(8,128)(2,1)} %get-tuple-element.127.y_ref, bf16[128,512]{1,0:T(8,128)(2,1)} %get-tuple-element.128.wide_ref, bf16[128,512]{1,0:T(8,128)(2,1)} %get-tuple-element.129.key_ref, ...), custom_call_target="tpu_custom_call" | custom-call | flops 3355443200 | bytes 20062208 | tf_op jit(solution)/shard_map/layer1_ask_back/pallas_call | solution.py:82
  80.5 10.7 %layer0_hidden_back.1 = (bf16[2,2112,512]{2,1,0:T(8,128)(2,1)}, bf16[1280,2048]{1,0:T(8,128)(2,1)}, f32[4,1,512]{2,1,0:T(1,128)}) custom-call(bf16[1280,512]{1,0:T(8,128)(2,1)} %get-tuple-element.143.low_ref, bf16[1280,2048]{1,0:T(8,128)(2,1)} %get-tuple-element.144.slope_ref, bf16[2,2048,512]{2,1,0:T(8,128)(2,1)} %wback_ref.7, ...), custom_call_target="tpu_custom_call" | custom-call | flops 5368709120 | bytes 21635072 | tf_op jit(solution)/shard_map/layer0_hidden_back/pallas_call | solution.py:82
  91.2 2.0 add_convert_fusion.1
  93.3 2.1 collective-permute-start.6
  95.4 11.3 %layer0_normed_back.1 = (bf16[2,2112,512]{2,1,0:T(8,128)(2,1)}, f32[1280,512]{1,0:T(8,128)}, bf16[1280,512]{1,0:T(8,128)(2,1)}, f32[8,512]{1,0:T(8,128)}) custom-call(bf16[1280,2048]{1,0:T(8,128)(2,1)} %get-tuple-element.157.dhidden_ref, f32[1280,512]{1,0:T(8,128)} %get-tuple-element.158.dmixed_ref, ...), custom_call_target="tpu_custom_call", output_to_operand_aliasing={{0}: (8, {})} | custom-call | flops 4026531840 | bytes 28991488 | tf_op jit(solution)/shard_map/layer0_normed_back/pallas_call | solution.py:82
  108.3 2.1 collective-permute-start.7
  110.4 16.8 %layer0_attention_back.1 = (bf16[1280,1536]{1,0:T(8,128)(2,1)}, bf16[2,2112,512]{2,1,0:T(8,128)(2,1)}) custom-call(bf16[1280,1536]{1,0:T(8,128)(2,1)} %get-tuple-element.174.qkv_ref, bf16[10,4,128,256]{3,2,1,0:T(8,128)(2,1)} %get-tuple-element.175.prob_ref, bf16[1280,512]{1,0:T(8,128)(2,1)} %get-tuple-element.176.dctx_ref, ...), custom_call_target="tpu_custom_call", output_to_operand_aliasing={{1}: (8, {})} | custom-call | flops 3690987520 | bytes 21798912 | tf_op jit(solution)/shard_map/layer0_attention_back/pallas_call | solution.py:82
  127.4 1.8 constant_dynamic-slice_fusion.2
  130.0 7.7 %layer0_input_back.1 = (f32[256,512]{1,0:T(8,128)}, f32[1024,512]{1,0:T(8,128)}) custom-call(bf16[1280,1536]{1,0:T(8,128)(2,1)} %get-tuple-element.189.dqkv_ref, f32[1280,512]{1,0:T(8,128)} %get-tuple-element.190.datt_ref, bf16[2,512,1536]{2,1,0:T(8,128)(2,1)} %wqkv_ref.7), custom_call_target="tpu_custom_call" | custom-call | flops 2013265920 | bytes 12320768 | tf_op jit(solution)/shard_map/layer0_input_back/pallas_call | solution.py:82
  137.7 4.1 %collective-permute-done.8 = bf16[448,512]{1,0:T(8,128)(2,1)} collective-permute-done((bf16[448,512]{1,0:T(8,128)(2,1)S(1)}, bf16[448,512]{1,0:T(8,128)(2,1)}, u32[]{:S(2)}, u32[]{:S(2)}) %collective-permute-start.8) | collective-permute-done | bytes 458784 | tf_op jit(solution)/shard_map/ppermute | solution.py:107
  142.9 2.2 add_convert_fusion
  147.7 4.5 %collective-permute-start.10 = (bf16[448,512]{1,0:T(8,128)(2,1)S(1)}, bf16[448,512]{1,0:T(8,128)(2,1)S(1)}, u32[]{:S(2)}, u32[]{:S(2)}) collective-permute-start(bf16[448,512]{1,0:T(8,128)(2,1)S(1)} %add_convert_fusion.8), channel_id=1, source_target_pairs={{0,12},{1,5},{2,14},{3,7},{4,8},{5,1},{6,10},{7,3},{8,4},{9,13},{1... | collective-permute-start | bytes 1376264 | tf_op jit(solution)/shard_map/ppermute | solution.py:107
  152.2 13.5 %top_grads.1 = (f32[2,512,512]{2,1,0:T(8,128)}, f32[2,512,2048]{2,1,0:T(8,128)}, f32[2,2048,512]{2,1,0:T(8,128)}, f32[8,512]{1,0:T(8,128)}, f32[1,2048]{1,0:T(1,128)}) custom-call(bf16[512,1024]{1,0:T(8,128)(2,1)} %bitcast.54, f32[512,512]{1,0:T(8,128)} %get-tuple-element.199.dy_ref, bf16[2,512,512]{2,1,0:T(8,128)(2,1)} %wout_ref.7, ...), custom_call_target="tpu_custom_call" | custom-call | flops 7247757312 | bytes 30482432 | tf_op jit(solution)/shard_map/top_grads/pallas_call | solution.py:82
  170.3 12.2 %collective-permute-done.12 = bf16[448,512]{1,0:T(8,128)(2,1)S(1)} collective-permute-done((bf16[448,512]{1,0:T(8,128)(2,1)}, bf16[448,512]{1,0:T(8,128)(2,1)S(1)}, u32[]{:S(2)}, u32[]{:S(2)}) %collective-permute-start.12) | collective-permute-done | bytes 458784 | tf_op jit(solution)/shard_map/ppermute | solution.py:107
  185.4 12.4 %collective-permute-done.15 = bf16[528,512]{1,0:T(8,128)(2,1)} collective-permute-done((bf16[528,512]{1,0:T(8,128)(2,1)S(1)}, bf16[528,512]{1,0:T(8,128)(2,1)}, u32[]{:S(2)}, u32[]{:S(2)}) %collective-permute-start.15) | collective-permute-done | bytes 540704 | tf_op jit(solution)/shard_map/ppermute | solution.py:107
  200.9 13.1 %collective-permute-done.17 = bf16[528,512]{1,0:T(8,128)(2,1)S(1)} collective-permute-done((bf16[528,512]{1,0:T(8,128)(2,1)S(1)}, bf16[528,512]{1,0:T(8,128)(2,1)S(1)}, u32[]{:S(2)}, u32[]{:S(2)}) %collective-permute-start.17) | collective-permute-done | bytes 540704 | tf_op jit(solution)/shard_map/ppermute | solution.py:107
  215.4 7.3 %unpack_first.1 = (f32[2,512,1536]{2,1,0:T(8,128)}, f32[2,2048,512]{2,1,0:T(8,128)}) custom-call(s32[1]{0:T(128)} %bitcast.bit_ref, bf16[1792,512]{1,0:T(8,128)(2,1)} %copy-done.2, bf16[1792,512]{1,0:T(8,128)(2,1)} %copy-done.4, f32[2,2048,512]{2,1,0:T(8,128)} %get-tuple-element.223._), custom_call_target="tpu_custom_call", output_to_operand_aliasing={{1}: (3, {})} | custom-call | bytes 11010048 | tf_op jit(solution)/shard_map/unpack_first/pallas_call | solution.py:648
  223.7 1.6 collective-permute-start.19
  225.3 13.6 %collective-permute-done.19 = bf16[1056,512]{1,0:T(8,128)(2,1)S(1)} collective-permute-done((bf16[1056,512]{1,0:T(8,128)(2,1)S(1)}, bf16[1056,512]{1,0:T(8,128)(2,1)S(1)}, u32[]{:S(2)}, u32[]{:S(2)}) %collective-permute-start.19) | collective-permute-done | bytes 1081376 | tf_op jit(solution)/shard_map/ppermute | solution.py:107
  239.5 4.2 %collective-permute-done.20.theirs_ref.theirs_v = bf16[2112,512]{1,0:T(8,128)(2,1)S(1)} collective-permute-done((bf16[2112,512]{1,0:T(8,128)(2,1)S(1)}, bf16[2112,512]{1,0:T(8,128)(2,1)S(1)}, u32[]{:S(2)}, u32[]{:S(2)}) %collective-permute-start.20) | collective-permute-done | bytes 2162720 | tf_op jit(solution)/shard_map/ppermute | solution.py:107
  245.2 6.1 %unpack_second.1 = (f32[2,512,2048]{2,1,0:T(8,128)}, f32[2,512,512]{2,1,0:T(8,128)}, f32[2,512,1536]{2,1,0:T(8,128)}, f32[2,1024]{1,0:T(2,128)}, f32[2,1024]{1,0...) custom-call(s32[1]{0:T(128)} %bitcast.bit_ref, ...), custom_call_target="tpu_custom_call", output_to_operand_aliasing={{0}: (7, {}), {1}: (8, {}), {2}: (9, {})} | custom-call | bytes 12582912 | tf_op jit(solution)/shard_map/unpack_second/pallas_call | solution.py:648
  (84 shorter events, 28.9 us)
Async XLA Ops:
  1.4 0.8 copy-start.7
  28.4 5.1 %collective-permute-start = (bf16[1,16,1024]{2,1,0:T(8,128)(2,1)}, bf16[1,16,1024]{2,1,0:T(8,128)(2,1)S(1)}, u32[]{:S(2)}, u32[]{:S(2)}) collective-permute-start(bf16[1,16,1024]{2,1,0:T(8,128)(2,1)} %bitcast.60), channel_id=1, source_target_pairs={{0,2},{1,3},{2,0},{3,1},{4,6},{5,7},{6,4},{7,5},{8,10},{9,11},{10,... | collective-permute-start | bytes 98312 | tf_op jit(solution)/shard_map/ppermute | solution.py:107
  34.2 4.4 %collective-permute-start.1 = (bf16[2,16,1024]{2,1,0:T(8,128)(2,1)S(1)}, bf16[2,16,1024]{2,1,0:T(8,128)(2,1)S(1)}, u32[]{:S(2)}, u32[]{:S(2)}) collective-permute-start(bf16[2,16,1024]{2,1,0:T(8,128)(2,1)S(1)} %maximum_bitcast_fusion.1), channel_id=1, source_target_pairs={{0,4},{1,5},{2,6},{3,7},{4,0},{5,1},{6,2},{7,3},{8,12},{9,13},{10,... | collective-permute-start | bytes 196616 | tf_op jit(solution)/shard_map/ppermute | solution.py:107
  38.7 6.1 %collective-permute-start.2 = (bf16[4,16,1024]{2,1,0:T(8,128)(2,1)S(1)}, bf16[4,16,1024]{2,1,0:T(8,128)(2,1)S(1)}, u32[]{:S(2)}, u32[]{:S(2)}) collective-permute-start(bf16[4,16,1024]{2,1,0:T(8,128)(2,1)S(1)} %bitcast.59), channel_id=1, source_target_pairs={{0,8},{1,9},{2,10},{3,11},{4,12},{5,13},{6,14},{7,15},{8,0},{9,1},... | collective-permute-start | bytes 393224 | tf_op jit(solution)/shard_map/ppermute | solution.py:107
  44.8 8.0 %copy-start.6 = (s32[256]{0:T(256)S(1)}, s32[256]{0:T(256)}, u32[]{:S(2)}) copy-start(s32[256]{0:T(256)} %param.18) | copy-start | bytes 3076
  44.8 7.6 %collective-permute-start.3 = (bf16[8,16,1024]{2,1,0:T(8,128)(2,1)S(1)}, bf16[8,16,1024]{2,1,0:T(8,128)(2,1)S(1)}, u32[]{:S(2)}, u32[]{:S(2)}) collective-permute-start(bf16[8,16,1024]{2,1,0:T(8,128)(2,1)S(1)} %bitcast.58), channel_id=1, source_target_pairs={{0,16},{1,17},{2,18},{3,19},{4,20},{5,21},{6,22},{7,23},{8,24},{9,... | collective-permute-start | bytes 786440 | tf_op jit(solution)/shard_map/ppermute | solution.py:107
  52.6 2.0 collective-permute-start.4
  80.3 10.9 %collective-permute-start.5 = (bf16[1792,512]{1,0:T(8,128)(2,1)S(1)}, bf16[1792,512]{1,0:T(8,128)(2,1)}, u32[]{:S(2)}, u32[]{:S(2)}) collective-permute-start(bf16[1792,512]{1,0:T(8,128)(2,1)S(1)} %constant_dynamic-slice_fusion.5), channel_id=1, source_target_pairs={{0,1},{1,0},{2,3},{3,2},{4,5},{5,4},{6,7},{7,6},{8,9},{9,8},{10,11... | collective-permute-start | bytes 5505032 | tf_op jit(solution)/shard_map/ppermute | solution.py:107
  80.5 10.7 %copy-start.3 = (bf16[3584,512]{1,0:T(8,128)(2,1)S(1)}, bf16[3584,512]{1,0:T(8,128)(2,1)}, u32[]{:S(2)}) copy-start(bf16[3584,512]{1,0:T(8,128)(2,1)} %get-tuple-element.138) | copy-start | bytes 11010052
  93.3 13.6 %collective-permute-start.6 = (bf16[896,512]{1,0:T(8,128)(2,1)S(1)}, bf16[896,512]{1,0:T(8,128)(2,1)}, u32[]{:S(2)}, u32[]{:S(2)}) collective-permute-start(bf16[896,512]{1,0:T(8,128)(2,1)S(1)} %constant_dynamic-slice_fusion.4), channel_id=1, source_target_pairs={{0,16},{1,3},{2,18},{3,1},{4,20},{5,7},{6,22},{7,5},{8,24},{9,11},... | collective-permute-start | bytes 2752520 | tf_op jit(solution)/shard_map/ppermute | solution.py:107
  108.3 18.9 %collective-permute-start.7 = (bf16[448,512]{1,0:T(8,128)(2,1)S(1)}, bf16[448,512]{1,0:T(8,128)(2,1)S(1)}, u32[]{:S(2)}, u32[]{:S(2)}) collective-permute-start(bf16[448,512]{1,0:T(8,128)(2,1)S(1)} %constant_dynamic-slice_fusion.3), channel_id=1, source_target_pairs={{0,2},{1,17},{2,0},{3,19},{4,6},{5,21},{6,4},{7,23},{8,10},{9,25},... | collective-permute-start | bytes 1376264 | tf_op jit(solution)/shard_map/ppermute | solution.py:107
  129.2 12.6 %collective-permute-start.9 = (bf16[2112,512]{1,0:T(8,128)(2,1)S(1)}, bf16[2112,512]{1,0:T(8,128)(2,1)}, u32[]{:S(2)}, u32[]{:S(2)}) collective-permute-start(bf16[2112,512]{1,0:T(8,128)(2,1)S(1)} %constant_dynamic-slice_fusion.2), channel_id=1, source_target_pairs={{0,1},{1,0},{2,3},{3,2},{4,5},{5,4},{6,7},{7,6},{8,9},{9,8},{10,11... | collective-permute-start | bytes 6488072 | tf_op jit(solution)/shard_map/ppermute | solution.py:107
  129.2 12.5 %collective-permute-start.8 = (bf16[448,512]{1,0:T(8,128)(2,1)S(1)}, bf16[448,512]{1,0:T(8,128)(2,1)}, u32[]{:S(2)}, u32[]{:S(2)}) collective-permute-start(bf16[448,512]{1,0:T(8,128)(2,1)S(1)} %add_convert_fusion.9), channel_id=1, source_target_pairs={{0,4},{1,13},{2,6},{3,15},{4,0},{5,9},{6,2},{7,11},{8,12},{9,5},{1... | collective-permute-start | bytes 1376264 | tf_op jit(solution)/shard_map/ppermute | solution.py:107
  130.0 12.9 %slice-start = ((s8[4325376]{0:T(1024)(128)(4,1)}), s8[131072]{0:T(1024)(128)(4,1)S(1)}, s32[]{:S(2)}) async-start(s8[4325376]{0:T(1024)(128)(4,1)} %bitcast.50), calls=%async_computation | async-start | bytes 262144
  130.0 12.9 %slice-start.1 = ((s8[4325376]{0:T(1024)(128)(4,1)}), s8[4194304]{0:T(1024)(128)(4,1)S(1)}, s32[]{:S(2)}) async-start(s8[4325376]{0:T(1024)(128)(4,1)} %bitcast.50), calls=%async_computation.1 | async-start | bytes 8388608
  146.2 19.5 %collective-permute-start.11 = (bf16[1056,512]{1,0:T(8,128)(2,1)}, bf16[1056,512]{1,0:T(8,128)(2,1)}, u32[]{:S(2)}, u32[]{:S(2)}) collective-permute-start(bf16[1056,512]{1,0:T(8,128)(2,1)} %constant_dynamic-slice_fusion.1), channel_id=1, source_target_pairs={{0,16},{1,3},{2,18},{3,1},{4,20},{5,7},{6,22},{7,5},{8,24},{9,11},... | collective-permute-start | bytes 3244040 | tf_op jit(solution)/shard_map/ppermute | solution.py:107
  147.7 18.0 %collective-permute-start.10 = (bf16[448,512]{1,0:T(8,128)(2,1)S(1)}, bf16[448,512]{1,0:T(8,128)(2,1)S(1)}, u32[]{:S(2)}, u32[]{:S(2)}) collective-permute-start(bf16[448,512]{1,0:T(8,128)(2,1)S(1)} %add_convert_fusion.8), channel_id=1, source_target_pairs={{0,12},{1,5},{2,14},{3,7},{4,8},{5,1},{6,10},{7,3},{8,4},{9,13},{1... | collective-permute-start | bytes 1376264 | tf_op jit(solution)/shard_map/ppermute | solution.py:107
  168.2 15.1 %collective-permute-start.13 = (bf16[528,512]{1,0:T(8,128)(2,1)S(1)}, bf16[528,512]{1,0:T(8,128)(2,1)S(1)}, u32[]{:S(2)}, u32[]{:S(2)}) collective-permute-start(bf16[528,512]{1,0:T(8,128)(2,1)S(1)} %constant_dynamic-slice_fusion), channel_id=1, source_target_pairs={{0,2},{1,17},{2,0},{3,19},{4,6},{5,21},{6,4},{7,23},{8,10},{9,25},... | collective-permute-start | bytes 1622024 | tf_op jit(solution)/shard_map/ppermute | solution.py:107
  168.8 13.8 %collective-permute-start.12 = (bf16[448,512]{1,0:T(8,128)(2,1)}, bf16[448,512]{1,0:T(8,128)(2,1)S(1)}, u32[]{:S(2)}, u32[]{:S(2)}) collective-permute-start(bf16[448,512]{1,0:T(8,128)(2,1)} %add_convert_fusion.7), channel_id=1, source_target_pairs={{0,2},{1,17},{2,0},{3,19},{4,6},{5,21},{6,4},{7,23},{8,10},{9,25},... | collective-permute-start | bytes 1376264 | tf_op jit(solution)/shard_map/ppermute | solution.py:107
  182.5 0.8 copy-start.5
  184.8 13.5 %collective-permute-start.14 = (bf16[896,512]{1,0:T(8,128)(2,1)S(1)}, bf16[896,512]{1,0:T(8,128)(2,1)S(1)}, u32[]{:S(2)}, u32[]{:S(2)}) collective-permute-start(bf16[896,512]{1,0:T(8,128)(2,1)S(1)} %pad_maximum_fusion.3), channel_id=1, source_target_pairs={{0,16},{1,3},{2,18},{3,1},{4,20},{5,7},{6,22},{7,5},{8,24},{9,11},... | collective-permute-start | bytes 2752520 | tf_op jit(solution)/shard_map/ppermute | solution.py:107
  185.4 12.4 %collective-permute-start.15 = (bf16[528,512]{1,0:T(8,128)(2,1)S(1)}, bf16[528,512]{1,0:T(8,128)(2,1)}, u32[]{:S(2)}, u32[]{:S(2)}) collective-permute-start(bf16[528,512]{1,0:T(8,128)(2,1)S(1)} %add_convert_fusion.6), channel_id=1, source_target_pairs={{0,4},{1,13},{2,6},{3,15},{4,0},{5,9},{6,2},{7,11},{8,12},{9,5},{1... | collective-permute-start | bytes 1622024 | tf_op jit(solution)/shard_map/ppermute | solution.py:107
  199.9 15.5 %copy-start.2 = (bf16[1792,512]{1,0:T(8,128)(2,1)}, bf16[1792,512]{1,0:T(8,128)(2,1)S(1)}, u32[]{:S(2)}) copy-start(bf16[1792,512]{1,0:T(8,128)(2,1)S(1)} %pad_maximum_fusion.1.mine_ref) | copy-start | bytes 5505028
  199.9 14.1 %collective-permute-start.16 = (bf16[1792,512]{1,0:T(8,128)(2,1)S(1)}, bf16[1792,512]{1,0:T(8,128)(2,1)S(1)}, u32[]{:S(2)}, u32[]{:S(2)}) collective-permute-start(bf16[1792,512]{1,0:T(8,128)(2,1)S(1)} %pad_maximum_fusion.1.mine_ref), channel_id=1, source_target_pairs={{0,1},{1,0},{2,3},{3,2},{4,5},{5,4},{6,7},{7,6},{8,9},{9,8},{10,11... | collective-permute-start | bytes 5505032 | tf_op jit(solution)/shard_map/ppermute | solution.py:107
  200.0 14.0 %collective-permute-start.17 = (bf16[528,512]{1,0:T(8,128)(2,1)S(1)}, bf16[528,512]{1,0:T(8,128)(2,1)S(1)}, u32[]{:S(2)}, u32[]{:S(2)}) collective-permute-start(bf16[528,512]{1,0:T(8,128)(2,1)S(1)} %add_convert_fusion.5), channel_id=1, source_target_pairs={{0,12},{1,5},{2,14},{3,7},{4,8},{5,1},{6,10},{7,3},{8,4},{9,13},{1... | collective-permute-start | bytes 1622024 | tf_op jit(solution)/shard_map/ppermute | solution.py:107
  214.0 1.5 copy-start.4
  214.1 9.4 %collective-permute-start.18 = (bf16[528,512]{1,0:T(8,128)(2,1)S(1)}, bf16[528,512]{1,0:T(8,128)(2,1)S(1)}, u32[]{:S(2)}, u32[]{:S(2)}) collective-permute-start(bf16[528,512]{1,0:T(8,128)(2,1)S(1)} %add_convert_fusion.4), channel_id=1, source_target_pairs={{0,2},{1,17},{2,0},{3,19},{4,6},{5,21},{6,4},{7,23},{8,10},{9,25},... | collective-permute-start | bytes 1622024 | tf_op jit(solution)/shard_map/ppermute | solution.py:107
  223.7 15.2 %collective-permute-start.19 = (bf16[1056,512]{1,0:T(8,128)(2,1)S(1)}, bf16[1056,512]{1,0:T(8,128)(2,1)S(1)}, u32[]{:S(2)}, u32[]{:S(2)}) collective-permute-start(bf16[1056,512]{1,0:T(8,128)(2,1)S(1)} %pad_maximum_fusion.2), channel_id=1, source_target_pairs={{0,16},{1,3},{2,18},{3,1},{4,20},{5,7},{6,22},{7,5},{8,24},{9,11},... | collective-permute-start | bytes 3244040 | tf_op jit(solution)/shard_map/ppermute | solution.py:107
  239.4 4.3 %copy-start = (bf16[2112,512]{1,0:T(8,128)(2,1)}, bf16[2112,512]{1,0:T(8,128)(2,1)S(1)}, u32[]{:S(2)}) copy-start(bf16[2112,512]{1,0:T(8,128)(2,1)S(1)} %pad_maximum_fusion.mine_ref.mine_v) | copy-start | bytes 6488068
  239.5 4.3 %collective-permute-start.20 = (bf16[2112,512]{1,0:T(8,128)(2,1)S(1)}, bf16[2112,512]{1,0:T(8,128)(2,1)S(1)}, u32[]{:S(2)}, u32[]{:S(2)}) collective-permute-start(bf16[2112,512]{1,0:T(8,128)(2,1)S(1)} %pad_maximum_fusion.mine_ref.mine_v), channel_id=1, source_target_pairs={{0,1},{1,0},{2,3},{3,2},{4,5},{5,4},{6,7},{7,6},{8,9},{9,8},{10,11... | collective-permute-start | bytes 6488072 | tf_op jit(solution)/shard_map/ppermute | solution.py:107
  243.8 1.4 copy-start.1
where the time goes:
time: 253 us; the launch traced here: 251 us
  Pallas kernels  122 us (48%)
  waiting for transfers between devices  73.8 us (29%)
  starting transfers between devices  29.5 us (12%)
  other arithmetic  15.1 us (6%)
  local copies, waits for them, and re-layouts  9.54 us (4%)
    pallas_call x9, Pallas kernels, kernel_call(): pl.pallas_call(body, grid=grid, in_specs=[s for _, s in ins], out_specs=[...  109 us
    ppermute x21, waiting for transfers between devices, swap(): lax.ppermute(value, AXES, [(i, i ^ (hop[1] if i & 1 else hop[0])) for i i...  73.8 us
    ppermute x21, starting transfers between devices, swap(): lax.ppermute(value, AXES, [(i, i ^ (hop[1] if i & 1 else hop[0])) for i i...  29.5 us
    pallas_call x2, Pallas kernels, unpack_call(): pl.pallas_call(body, grid_spec=pltpu.PrefetchScalarGridSpec(num_scalar_pr...  13.4 us
    convert_element_type x6, other arithmetic, sum_steps(): cur = (mine.astype(F32) + got.astype(F32)).astype(BF)  7.46 us
  transfers between devices with their start and end apart: 21, of which 14 were waited for; matrix products, arithmetic and copies ran while one was open for 0% of the time, Pallas kernels for 27%

commit v1 on v0

v1 whole, which is shorter than its diff:
```python
import functools
import math

import jax
import jax.numpy as jnp
from jax import lax
from jax.experimental import pallas as pl
from jax.experimental.pallas import tpu as pltpu
from jax.sharding import PartitionSpec as P

HEADS = 8
BF = jnp.bfloat16
F32 = jnp.float32
AXES = ("stream", "dp")
logit_scale = 40.0
margin = 0.3
norm_eps = 1e-12
unit_eps = 1e-06
BLOCK = 128
STEP = 256
VMEM = 30 * 1024 * 1024


def mm(a, b):
    return jnp.dot(a, b, preferred_element_type=F32)


def mm_nt(a, b):
    return lax.dot_general(a, b, (((1,), (1,)), ((), ())), preferred_element_type=F32)


def mm_tn(a, b):
    return lax.dot_general(a, b, (((0,), (0,)), ((), ())), preferred_element_type=F32)


def ln_stats(v):
    centre = v - jnp.mean(v, -1, keepdims=True)
    rstd = lax.rsqrt(jnp.mean(centre * centre, -1, keepdims=True) + norm_eps)
    return centre * rstd, rstd


def ln_back(dy, vhat, rstd, gain):
    dhat = dy * gain
    return (dhat - jnp.mean(dhat, -1, keepdims=True) - vhat * jnp.mean(dhat * vhat, -1, keepdims=True)) * rstd


def gelu_pair(v):
    cdf = 0.5 * (1.0 + lax.erf(v * (1.0 / math.sqrt(2.0))))
    pdf = jnp.exp(-0.5 * v * v) * (1.0 / math.sqrt(2.0 * math.pi))
    return v * cdf, cdf + v * pdf


def colsum(v):
    return jnp.sum(v.astype(F32), 0)


def rowsum(v):
    return jnp.sum(v.astype(F32), 0, keepdims=True)


SMEM = pl.BlockSpec(memory_space=pltpu.SMEM)
ANY = pl.BlockSpec(memory_space=pl.ANY)


def hbm(a):
    return pltpu.with_memory_space_constraint(a, memory_space=pltpu.HBM)


def hbm_shape(dims, dtype):
    return pltpu.HBM(dims, dtype)


def whole(a):
    return pl.BlockSpec(a.shape, lambda i: (0,) * len(a.shape))


def shape(dims, dtype):
    return jax.ShapeDtypeStruct(dims, dtype)


def layer_of(a, level, rows=None, cols=None, at=lambda i: (0, 0)):
    rows, cols = rows or a.shape[1], cols or a.shape[2]
    return a, pl.BlockSpec((None, rows, cols), lambda i: (level, *at(i)))


def kernel_call(body, name, grid, ins, outs, flops, scratch=(), aliases=None, vmem=VMEM):
    size = sum(a.size * a.dtype.itemsize for a, _ in ins) + sum(
        math.prod(s.shape) * jnp.dtype(s.dtype).itemsize for s, _ in outs
    )
    return pl.pallas_call(
        body,
        grid=grid,
        in_specs=[s for _, s in ins],
        out_specs=[s for _, s in outs],
        out_shape=[s for s, _ in outs],
        scratch_shapes=list(scratch),
        input_output_aliases=aliases or {},
        compiler_params=pltpu.CompilerParams(vmem_limit_bytes=vmem),
        cost_estimate=pl.CostEstimate(flops=int(flops), bytes_accessed=int(size), transcendentals=0),
        name=name,
    )(*[hbm(a) if s is ANY else a for a, s in ins])


def routes(n):
    top, y = n >> 1, 2
    rest = [1 << k for k in range(2, n.bit_length() - 2)]
    for k in range(1, len(rest)):
        rest[k] |= rest[k - 1]
    halved = [(1, 1), (top, y), (y, top)]
    added = list(zip(rest, rest[::-1]))
    return halved, added


def swap(value, n, hop):
    return lax.ppermute(value, AXES, [(i, i ^ (hop[1] if i & 1 else hop[0])) for i in range(n)])


def device_index():
    return lax.axis_index("stream") * lax.axis_size("dp") + lax.axis_index("dp")


def coordinate(index, hop, n):
    value = (index // (1 << (hop.bit_length() - 1))) % 2
    if hop in (1, 2, n >> 1) or 2 * hop >= n >> 1:
        return value
    above = (index // (1 << hop.bit_length())) % 2
    return value + above - 2 * value * above


def my_bits(n):
    index = device_index()
    core = index % 2
    halved, _ = routes(n)
    return [jnp.where(core == 0, coordinate(index, a, n), coordinate(index, b, n)) for a, b in halved]


def split_body(bit_ref, mine_a, got_a, mine_b, got_b, keep_ref, send_ref):
    keep_ref[...] = (mine_a[...].astype(F32) + got_a[...].astype(F32)).astype(BF)
    send_ref[...] = (mine_b[...].astype(F32) + got_b[...].astype(F32)).astype(BF)


def add_and_split(mine, got, bit):
    rows, width = mine.shape[0] // 2, mine.shape[1]
    steps = 2 if rows % 32 == 0 and rows >= 256 else 1
    block = rows // steps
    kept = pl.BlockSpec((block, width), lambda j, bit: (bit[0] * steps + j, 0))
    sent = pl.BlockSpec((block, width), lambda j, bit: ((1 - bit[0]) * steps + j, 0))
    out = pl.BlockSpec((block, width), lambda j, bit: (j, 0))
    ins = [(mine, kept), (got, kept), (mine, sent), (got, sent)]
    outs = [(shape((rows, width), BF), out)] * 2
    return unpack_call(split_body, "add_and_split", bit.reshape(1).astype(jnp.int32), (steps,), ins, outs, {}, 12 * rows * width)


def sum_steps(keep, send, n, bits):
    halved, added = routes(n)
    for k, hop in enumerate(halved[:-1]):
        got = yield send, hop
        keep, send = add_and_split(keep, got, bits[k + 1])
    got = yield send, halved[-1]
    cur = (keep.astype(F32) + got.astype(F32)).astype(BF)
    for hop in added:
        got = yield cur, hop
        cur = (cur.astype(F32) + got.astype(F32)).astype(BF)
    for hop, bit in reversed(list(zip(halved, bits))[1:]):
        got = yield cur, hop
        low = jnp.where(bit == 0, cur, got)
        high = jnp.where(bit == 0, got, cur)
        cur = jnp.concatenate([low, high], 0)
    got = yield cur, halved[0]
    return cur, got


class Lane:
    def __init__(self, steps, n):
        self.n, self.steps, self.result = n, steps, None
        self.ask = next(self.steps)

    def feed(self, got):
        try:
            self.ask = self.steps.send(got)
        except StopIteration as end:
            self.result = end.value


def stage(lanes, work=None, args=()):
    lanes = [lane for lane in lanes if lane.result is None]
    asked, args = lax.optimization_barrier(([lane.ask[0] for lane in lanes], args))
    got = [swap(value, lane.n, lane.ask[1]) for value, lane in zip(asked, lanes)]
    out = work(*args) if work else ()
    got, out = lax.optimization_barrier((got, out))
    for lane, value in zip(lanes, got):
        lane.feed(value)
    return out


def gather_rows(rows, n):
    index = device_index()
    cur = rows[None]
    for flip in [1 << k for k in range(1, n.bit_length() - 1)] + [1]:
        got = swap(cur, n, (flip, flip))
        bit = (index // flip) % 2
        low, high = jnp.where(bit == 0, cur, got), jnp.where(bit == 0, got, cur)
        cur = jnp.stack([low, high], 1 if flip == 1 else 0).reshape((2 * cur.shape[0],) + rows.shape)
    return cur.reshape(n * rows.shape[0], rows.shape[1])


def stream_in(pairs, sems):
    loads = [pltpu.make_async_copy(a, b, sems.at[k]) for k, (a, b) in enumerate(pairs)]
    for load in loads:
        load.start()
    return loads


class Halves:
    def __init__(self, keep, send, block, sems):
        self.keep, self.send, self.block, self.sems = keep, send, block, sems
        self.low_is_kept = lax.axis_index("dp") % 2 == 0
        self.pieces = 0
        self.waits = []

    def put(self, at, value):
        self.block[at : at + value.shape[0]] = value
        half = self.keep.shape[0]
        end = at + value.shape[0]
        for lower, a, b in ((True, at, min(end, half)), (False, max(at, half), end)):
            if a >= b:
                continue
            base = 0 if lower else half
            sem = self.sems.at[self.pieces]
            self.pieces += 1
            copies = [
                pltpu.make_async_copy(self.block.at[a:b], ref.at[a - base : b - base], sem) for ref in (self.keep, self.send)
            ]
            kept = self.low_is_kept if lower else jnp.logical_not(self.low_is_kept)

            @pl.when(kept)
            def _(copy=copies[0]):
                copy.start()

            @pl.when(jnp.logical_not(kept))
            def _(copy=copies[1]):
                copy.start()

            self.waits.append(copies[0])

    def finish(self):
        for copy in self.waits:
            copy.wait()


def halves(v, first):
    zero = jnp.zeros_like(v)
    return jnp.concatenate([jnp.where(first, v, zero), jnp.where(first, zero, v)], 0)


def join_halves(v, first):
    return jnp.where(first, v[: v.shape[0] // 2], v[v.shape[0] // 2 :])


def first_head(width):
    return lax.broadcasted_iota(jnp.int32, (1, 2 * width // HEADS), 1) < width // HEADS


def key_bias(lens_ref, block, span_short, count_short):
    key = lax.broadcasted_iota(jnp.int32, (BLOCK, 1), 0)
    query = lax.broadcasted_iota(jnp.int32, (1, BLOCK), 1)
    per = BLOCK // span_short
    blocks_short = count_short // per
    is_short = block < blocks_short
    at = jnp.where(is_short, block * per, count_short + block - blocks_short)
    limit = jnp.zeros((BLOCK, 1), jnp.int32)
    for s in range(per):
        inside = key // span_short == s
        limit = jnp.where(inside, jnp.where(is_short, lens_ref[at + jnp.where(is_short, s, 0)] + s * span_short, 0), limit)
    limit = jnp.where(is_short, limit, lens_ref[at])
    same = (key // span_short == query // span_short) | jnp.logical_not(is_short)
    return jnp.where((key < limit) & same, 0.0, -jnp.inf).astype(F32)


def vectors(level, width, bqv_ref, bresid_ref, gain_ref, shift_ref):
    row = slice(level, level + 1)
    low, high = slice(0, width), slice(width, 2 * width)
    return [ref[row, part] for ref in (bqv_ref, bresid_ref, gain_ref, shift_ref) for part in (low, high)]


def forward_body(
    span, count, lens_ref, short_ref, long_ref, wqkv_ref, wout_ref, win_ref, wback_ref, bin_ref, bqv_ref, bresid_ref, gain_ref, shift_ref,
    y_ref, qkv_ref, prob_ref, ctx_ref, hat1_ref, rstd1_ref, act_ref, slope_ref, hat2_ref, rstd2_ref,
):
    step = pl.program_id(0)
    x = jnp.where(step == 0, short_ref[...], long_ref[...])
    rows, width = x.shape
    bq, bv, bo, bb, g1, g2, c1, c2 = vectors(0, width, bqv_ref, bresid_ref, gain_ref, shift_ref)
    pair = 2 * width // HEADS
    first = first_head(width)
    scale = 1.0 / math.sqrt(width // HEADS)
    bias = jnp.concatenate([bq, jnp.zeros_like(bq), bv], 1)
    qkv = (mm(x, wqkv_ref[...]) + bias).astype(BF)
    qkv_ref[...] = qkv
    blocks = []
    for b in range(rows // BLOCK):
        r = slice(b * BLOCK, (b + 1) * BLOCK)
        hide = key_bias(lens_ref, step * (rows // BLOCK) + b, span, count)
        hide = jnp.concatenate([hide, hide], 1)
        cols = []
        for p in range(HEADS // 2):
            q, k, v = (qkv[r, m * width + p * pair : m * width + (p + 1) * pair] for m in range(3))
            logit = mm_nt(k, halves(q, first)) * scale + hide
            power = jnp.exp(logit - jnp.max(logit, 0, keepdims=True))
            prob = (power * (1.0 / jnp.sum(power, 0, keepdims=True))).astype(BF)
            prob_ref[b, p] = prob
            cols.append(join_halves(mm_tn(prob, v), first))
        blocks.append(jnp.concatenate(cols, 1).astype(BF))
    ctx = jnp.concatenate(blocks, 0)
    ctx_ref[...] = ctx
    hat1, rstd1 = ln_stats(x.astype(F32) + mm(ctx, wout_ref[...]) + bo)
    normed = hat1 * g1 + c1
    low = normed.astype(BF)
    hat1_ref[...] = hat1.astype(BF)
    rstd1_ref[...] = jnp.broadcast_to(rstd1, rstd1_ref.shape)
    act, slope = gelu_pair(mm(low, win_ref[...]) + bin_ref[0:1])
    act = act.astype(BF)
    act_ref[...] = act
    slope_ref[...] = slope.astype(BF)
    hat2, rstd2 = ln_stats(normed + mm(act, wback_ref[...]) + bb)
    hat2_ref[...] = hat2.astype(BF)
    rstd2_ref[...] = jnp.broadcast_to(rstd2, rstd2_ref.shape)
    y_ref[...] = (hat2 * g2 + c2).astype(BF)


def by_rows(cols):
    return pl.BlockSpec((STEP, cols), lambda i: (i, 0))


def from_buckets(short, long):
    width = short.shape[1]
    return [
        (short, pl.BlockSpec((STEP, width), lambda i: (0, 0))),
        (long, pl.BlockSpec((STEP, width), lambda i: (jnp.maximum(i - 1, 0), 0))),
    ]


def small_ins(w):
    return [(w[k], whole(w[k])) for k in ("b_qv", "b_resid", "gain", "shift")]


def forward(short, long, lens, w, span, count):
    rows, width = short.shape[0] + long.shape[0], short.shape[1]
    ff = w["in"].shape[2]
    per = STEP // BLOCK
    prob = pl.BlockSpec((per, HEADS // 2, BLOCK, 2 * BLOCK), lambda i: (i, 0, 0, 0))
    ins = [(lens, SMEM)] + from_buckets(short, long)
    ins += [layer_of(w[name], 0) for name in ("qkv", "out", "in", "back")] + [(w["b_in"], whole(w["b_in"]))] + small_ins(w)
    far = [False] + [True] * 9
    cols = [(width, BF), (3 * width, BF), None, (width, BF), (width, BF), (128, F32), (ff, BF), (ff, BF), (width, BF), (128, F32)]
    outs = [((hbm_shape if f else shape)((rows, c[0]), c[1]), by_rows(c[0])) if c else (hbm_shape((rows // BLOCK, HEADS // 2, BLOCK, 2 * BLOCK), BF), prob) for c, f in zip(cols, far)]
    body = functools.partial(forward_body, span, count)
    return kernel_call(body, "layer0_forward", (rows // STEP,), ins, outs, 2 * rows * width * (4 * width + 2 * ff))


def starts(sents, spans, rows):
    s = lax.broadcasted_iota(jnp.int32, (sents, rows), 0)
    r = lax.broadcasted_iota(jnp.int32, (sents, rows), 1)
    half = sents // 2
    at = jnp.where(s < half, s * spans[0], half * spans[0] + (s - half) * spans[1])
    return (r == at).astype(BF)


def spread(sents):
    a = lax.broadcasted_iota(jnp.int32, (sents * HEADS, sents), 0) // HEADS
    return (a == lax.broadcasted_iota(jnp.int32, (sents * HEADS, sents), 1)).astype(BF)


def own_head(sents, width):
    a = lax.broadcasted_iota(jnp.int32, (sents * HEADS, width), 0) % HEADS
    return a == lax.broadcasted_iota(jnp.int32, (sents * HEADS, width), 1) // (width // HEADS)


def sum_heads(v, keep, sents):
    return jnp.sum(jnp.where(keep, v, 0.0).reshape(sents, HEADS, v.shape[1]), 1)


def ask_body(spans, y_ref, lens_ref, wqkv_ref, bqv_ref, wout_ref, bresid_ref, out_ref, ctx_ref, wide_ref, key_ref, prob_ref, mixed_ref):
    y = y_ref[...]
    rows, width = y.shape
    sents = out_ref.shape[0]
    keep = own_head(sents, width)
    cls = mm(starts(sents, spans, rows), y).astype(BF)
    q = (mm(cls, wqkv_ref[:, :width]) + bqv_ref[1:2, :width]).astype(BF)
    wide = jnp.where(keep, mm(spread(sents), q), 0.0).astype(BF)
    key = mm_nt(wide, wqkv_ref[:, width : 2 * width]).astype(BF)
    half = sents // 2
    sent = lax.broadcasted_iota(jnp.int32, (sents * HEADS, 1), 0) // HEADS
    begin = jnp.where(sent < half, sent * spans[0], half * spans[0] + (sent - half) * spans[1])
    place = lax.broadcasted_iota(jnp.int32, (sents * HEADS, rows), 1) - begin
    seen = (place >= 0) & (place < lens_ref[...])
    logit = jnp.where(seen, mm_nt(key, y) * (1.0 / math.sqrt(width // HEADS)), -jnp.inf)
    power = jnp.exp(logit - jnp.max(logit, 1, keepdims=True))
    prob = (power * (1.0 / jnp.sum(power, 1, keepdims=True))).astype(BF)
    mixed = mm(prob, y).astype(BF)
    picked = sum_heads(mm(mixed, wqkv_ref[:, 2 * width :]), keep, sents)
    ctx = (picked + bqv_ref[1:2, width:]).astype(BF)
    ctx_ref[...] = ctx
    out_ref[...] = (cls.astype(F32) + mm(ctx, wout_ref[...]) + bresid_ref[1:2, :width]).astype(BF)
    wide_ref[...] = wide
    key_ref[...] = key
    prob_ref[...] = prob
    mixed_ref[...] = mixed


def ask(y, lens, w, spans, sents):
    rows, width = y.shape
    wide = sents * HEADS
    ins = [(y, whole(y)), (lens, whole(lens)), layer_of(w["qkv"], 1), (w["b_qv"], whole(w["b_qv"])), layer_of(w["out"], 1), (w["b_resid"], whole(w["b_resid"]))]
    outs = [(s, whole(s)) for s in [shape((sents, width), BF)] + [hbm_shape(d, BF) for d in ((sents, width), (wide, width), (wide, width), (wide, rows), (wide, width))]]
    return kernel_call(functools.partial(ask_body, spans), "layer1_ask", (1,), ins, outs, 2 * wide * width * (2 * rows + 3 * width))


def top_forward(attended, win_ref, bin_ref, g1, c1):
    hat1, rstd1 = ln_stats(attended.astype(F32))
    normed = hat1 * g1 + c1
    low = normed.astype(BF)
    return hat1, rstd1, normed, low, mm(low, win_ref[...]) + bin_ref[1:2]


def gelu(v):
    return v * (0.5 * (1.0 + lax.erf(v * (1.0 / math.sqrt(2.0)))))


def top_part(index_ref, every_ref, pair_ref, dy_ref, hat2_s, rstd2_s, low_vectors, bin_ref, win, wback, wout_ref, sents):
    pairs = pair_ref.shape[1]
    _, _, _, bb, g1, g2, c1, c2 = low_vectors
    hat1, _ = ln_stats(every_ref[...].astype(F32))
    normed = hat1 * g1 + c1
    win_ref = win()
    act = gelu(mm(normed.astype(BF), win_ref[...]) + bin_ref[1:2]).astype(BF)
    wback_ref = wback()
    hat2, rstd2 = ln_stats(normed + mm(act, wback_ref[...]) + bb)
    hat2_s[...] = hat2
    rstd2_s[...] = jnp.broadcast_to(rstd2, rstd2_s.shape)
    pooled = hat2 * g2 + c2
    radius = lax.rsqrt(jnp.sum(pooled * pooled, -1, keepdims=True) + unit_eps)
    unit = pooled * radius
    src, tgt = unit[:pairs].astype(BF), unit[pairs:].astype(BF)
    positive = (pair_ref[...] == lax.broadcasted_iota(jnp.int32, (pairs, pairs), 0)).astype(F32)
    logits = logit_scale * (mm_nt(tgt, src) - margin * positive)

    def soft(axis):
        powers = jnp.exp(logits - jnp.max(logits, axis, keepdims=True))
        return powers * (1.0 / jnp.sum(powers, axis, keepdims=True))

    dscore = (0.5 * logit_scale * (soft(1) + soft(0) - 2.0 * positive)).astype(BF)
    dunit = jnp.concatenate([mm_tn(dscore, tgt), mm(dscore, src)], 0)
    dy_ref[...] = radius * (dunit - unit * jnp.sum(dunit * unit, -1, keepdims=True))
    mine = pl.ds(pl.multiple_of(index_ref[0] * sents, sents), sents)
    own_hat1, own_rstd1, _, _, own_hid = top_forward(every_ref[mine], win_ref, bin_ref, g1, c1)
    dmixed = ln_back(dy_ref[mine], hat2_s[mine], rstd2_s[mine, 0:1], g2)
    dhidden = (mm_nt(dmixed.astype(BF), wback_ref[...]) * gelu_pair(own_hid)[1]).astype(BF)
    dnormed = dmixed + mm_nt(dhidden, win_ref[...])
    datt = ln_back(dnormed, own_hat1, own_rstd1, g1)
    return datt, mm_nt(datt.astype(BF), wout_ref[...]).astype(BF)


def top_grads_body(every_ref, dy_ref, wout_ref, win_ref, wback_ref, bin_ref, bqv_ref, bresid_ref, gain_ref, shift_ref,
                   gin_ref, gback_ref, sums_ref, sumin_ref):
    width = dy_ref.shape[1]
    _, _, _, bb, g1, g2, c1, c2 = vectors(1, width, bqv_ref, bresid_ref, gain_ref, shift_ref)
    hat1, rstd1, normed, low, hid = top_forward(every_ref[...], win_ref, bin_ref, g1, c1)
    act, slope = gelu_pair(hid)
    act = act.astype(BF)
    hat2, rstd2 = ln_stats(normed + mm(act, wback_ref[...]) + bb)
    dy = dy_ref[...]
    dmixed = ln_back(dy, hat2, rstd2, g2)
    dmixed_low = dmixed.astype(BF)
    gback_ref[...] = mm_tn(act, dmixed_low)
    dhidden = (mm_nt(dmixed_low, wback_ref[...]) * slope).astype(BF)
    gin_ref[...] = mm_tn(low, dhidden)
    dnormed = dmixed + mm_nt(dhidden, win_ref[...])
    datt = ln_back(dnormed, hat1, rstd1, g1)
    sumin_ref[...] = rowsum(dhidden)
    parts = (datt, dmixed, dnormed * hat1, dy * hat2, dnormed, dy, mm_nt(datt.astype(BF), wout_ref[...]).astype(BF))
    for k, part in enumerate(parts):
        sums_ref[k : k + 1] = rowsum(part)
    sums_ref[7:8] = jnp.zeros((1, width), F32)


def top_grads(every, dy, w):
    width = dy.shape[1]
    ff = w["in"].shape[2]
    rows = every.shape[0]
    ins = [(every, whole(every)), (dy, whole(dy))] + [layer_of(w[k], 1) for k in ("out", "in", "back")]
    ins += [(w["b_in"], whole(w["b_in"]))] + small_ins(w)

    def upper(a, b):
        return hbm_shape((2, a, b), F32), pl.BlockSpec((None, a, b), lambda i: (1, 0, 0))

    sums, sumin = shape((8, width), F32), shape((1, ff), F32)
    outs = [upper(width, ff), upper(ff, width), (sums, whole(sums)), (sumin, whole(sumin))]
    return kernel_call(top_grads_body, "top_grads", (1,), ins, outs, 6 * rows * width * (width + 2 * ff))


def turn_body(spans, sents, with_top, *refs):
    refs = list(refs)

    def take(count):
        out, refs[:count] = refs[:count], []
        return out

    wide_ref, key_ref, prob_ref, mixed_ref, ctx_ref, gain_ref = take(6)
    wqkv_hbm, y_hbm, hat2_hbm, rstd2_hbm, act_hbm = take(5)
    if with_top:
        index_ref, every_ref, pair_ref, wout_ref, bin_ref, bqv_ref, bresid_ref, shift_ref, win_hbm, wback_hbm = take(10)
    else:
        datt_ref, dctx_ref = take(2)
    keep_hbm, send_hbm, low_ref, sums_ref = take(4)
    if with_top:
        (dy_ref,) = take(1)
    wqkv_ref, y_ref, hat2_ref, rstd2_ref, act_ref, block, got, sent = take(8)
    loads = [(wqkv_hbm.at[1], wqkv_ref), (y_hbm, y_ref), (hat2_hbm, hat2_ref), (rstd2_hbm, rstd2_ref), (act_hbm, act_ref)]
    if with_top:
        win_ref, wback_ref, top_hat2, top_rstd2 = take(4)
        loads = [(win_hbm.at[1], win_ref), (wback_hbm.at[1], wback_ref)] + loads
    loads = [pltpu.make_async_copy(a, b, got.at[k]) for k, (a, b) in enumerate(loads)]
    for load in loads:
        load.start()
    rows, width = y_ref.shape
    if with_top:

        def arrived(load, ref):
            def wait():
                load.wait()
                return ref

            return wait

        values = vectors(1, width, bqv_ref, bresid_ref, gain_ref, shift_ref)
        win, wback = arrived(loads[0], win_ref), arrived(loads[1], wback_ref)
        datt, dctx = top_part(index_ref, every_ref, pair_ref, dy_ref, top_hat2, top_rstd2, values, bin_ref, win, wback, wout_ref, sents)
        loads = loads[2:]
    else:
        datt, dctx = datt_ref[...], dctx_ref[...]
    keep = own_head(sents, width)
    first = starts(sents, spans, rows)
    prob_low = prob_ref[...]
    d_wide = jnp.where(keep, mm(spread(sents), dctx), 0.0).astype(BF)
    loads[0].wait()
    d_value = mm_nt(d_wide, wqkv_ref[:, 2 * width :]).astype(BF)
    loads[1].wait()
    y = y_ref[...]
    dprob = mm_nt(d_value, y)
    prob = prob_low.astype(F32)
    dlogit = prob * (dprob - jnp.sum(prob * dprob, 1, keepdims=True))
    dscore = (dlogit * (1.0 / math.sqrt(width // HEADS))).astype(BF)
    pulled = mm(dscore, y).astype(BF)
    dq = sum_heads(mm(pulled, wqkv_ref[:, width : 2 * width]), keep, sents).astype(BF)
    dcls = mm_nt(dq, wqkv_ref[:, :width]) + datt
    high = dcls.astype(BF)
    left = jnp.concatenate([dscore, prob_low, first, first], 0)
    right = jnp.concatenate([key_ref[...], d_value, high, (dcls - high.astype(F32)).astype(BF)], 0)
    dy = mm_tn(left, right)
    loads[2].wait()
    loads[3].wait()
    hat2 = hat2_ref[...].astype(F32)
    dmixed = ln_back(dy, hat2, rstd2_ref[:, 0:1], gain_ref[0:1, width:])
    low_ref[...] = dmixed.astype(BF)
    sums_ref[0:1] = rowsum(dmixed)
    sums_ref[1:2] = rowsum(dy * hat2)
    sums_ref[2:3] = rowsum(dy)
    sums_ref[3:4] = rowsum(dq)
    sums_ref[4:8] = jnp.zeros((4, width), F32)
    place = Halves(keep_hbm, send_hbm, block, sent)
    ff = act_ref.shape[1]
    tiles = ff // width
    cls = mm(first, y).astype(BF)
    tail = ((cls, dq), (pulled, wide_ref[...]), (mixed_ref[...], d_wide), (ctx_ref[...], datt.astype(BF)))
    for k, (a, b) in enumerate(tail):
        place.put((tiles + k) * width, mm_tn(a, b).astype(BF))
    loads[4].wait()
    for k in range(tiles):
        place.put(k * width, mm_tn(act_ref[:, k * width : (k + 1) * width], low_ref[...]).astype(BF))
    place.finish()


def turn(top_args, y, kept, w, hat2, rstd2, act, spans, sents):
    rows, width = y.shape
    ff = act.shape[1]
    ctx, wide, key, prob, mixed = kept
    with_top = len(top_args) == 3
    ins = [(a, whole(a)) for a in (wide, key, prob, mixed, ctx, w["gain"])]
    ins += [(a, ANY) for a in (w["qkv"], y, hat2, rstd2, act)]
    blocks = ff // width + 4
    outs = [(hbm_shape((blocks * width // 2, width), BF), ANY)] * 2
    outs += [(s, whole(s)) for s in (shape((rows, width), BF), shape((8, width), F32))]
    scratch = [pltpu.VMEM(d, t) for d, t in (((width, 3 * width), BF), ((rows, width), BF), ((rows, width), BF), ((rows, 128), F32), ((rows, ff), BF), ((blocks * width, width), BF))]
    scratch += [pltpu.SemaphoreType.DMA((7,)), pltpu.SemaphoreType.DMA((blocks,))]
    flops = 2 * rows * width * (ff + 512)
    if with_top:
        index, every, pair = top_args
        ins += [(index, SMEM), (every, whole(every)), (pair, whole(pair)), layer_of(w["out"], 1)]
        ins += [(w[k], whole(w[k])) for k in ("b_in", "b_qv", "b_resid", "shift")] + [(w["in"], ANY), (w["back"], ANY)]
        outs += [(hbm_shape(every.shape, F32), whole(every))]
        scratch += [pltpu.VMEM((width, ff), BF), pltpu.VMEM((ff, width), BF), pltpu.VMEM(every.shape, F32), pltpu.VMEM((every.shape[0], 128), F32)]
        flops += 4 * every.shape[0] * width * ff
    else:
        ins += [(a, whole(a)) for a in top_args]
    return kernel_call(functools.partial(turn_body, spans, sents, with_top), "turn", (1,), ins, outs, flops, scratch, vmem=VMEM + VMEM // 4)


VECTOR_ROWS = 128


def ff_back_body(low_ref, gain_ref, shift_ref, hat1_hbm, rstd1_hbm, wback_hbm, slope_hbm, win_hbm, wout_hbm, ctx_hbm,
                 keep_hbm, send_hbm, datt_ref, dctx_ref, sums_ref, sumin_ref,
                 hat1_ref, rstd1_ref, wback_ref, slope_ref, win_ref, wout_ref, ctx_ref, nlow_ref, dhidden_ref, block, got, sent):
    rows, width = low_ref.shape
    ff = slope_ref.shape[1]
    tiles = ff // width
    loads = [(hat1_hbm, hat1_ref)]
    for t in range(tiles):
        part = slice(t * width, (t + 1) * width)
        loads += [(wback_hbm.at[0, part], wback_ref.at[part]), (slope_hbm.at[:, part], slope_ref.at[:, part])]
    loads += [(win_hbm.at[0], win_ref), (rstd1_hbm, rstd1_ref), (wout_hbm.at[0], wout_ref), (ctx_hbm, ctx_ref)]
    loads = stream_in(loads, got)
    place = Halves(keep_hbm, send_hbm, block, sent)
    gain, shift = gain_ref[0:1, :width], shift_ref[0:1, :width]
    loads[0].wait()
    nlow_ref[...] = (hat1_ref[...].astype(F32) * gain + shift).astype(BF)
    for t in range(tiles):
        part = slice(t * width, (t + 1) * width)
        loads[1 + 2 * t].wait()
        loads[2 + 2 * t].wait()
        dhidden = (mm_nt(low_ref[...], wback_ref[part]) * slope_ref[:, part].astype(F32)).astype(BF)
        dhidden_ref[:, part] = dhidden
        sumin_ref[:, part] = rowsum(dhidden)
        place.put(t * width, mm_tn(nlow_ref[...], dhidden).astype(BF))
    for load in loads[1 + 2 * tiles :]:
        load.wait()
    sums_ref[...] = jnp.zeros_like(sums_ref)
    for r in range(0, rows, STEP):
        r = slice(r, r + STEP)
        dnormed = low_ref[r].astype(F32) + mm_nt(dhidden_ref[r], win_ref[...])
        hat1 = hat1_ref[r].astype(F32)
        datt = ln_back(dnormed, hat1, rstd1_ref[r, 0:1], gain)
        low = datt.astype(BF)
        datt_ref[r] = low
        dctx_ref[r] = mm_nt(low, wout_ref[...]).astype(BF)
        sums_ref[0:1] += rowsum(datt)
        sums_ref[1:2] += rowsum(dnormed * hat1)
        sums_ref[2:3] += rowsum(dnormed)
    place.put(ff, mm_tn(ctx_ref[...], datt_ref[...]).astype(BF))
    place.finish()


def ff_back(low, hat1, rstd1, slope, ctx, w):
    rows, width = low.shape
    ff = slope.shape[1]
    ins = [(low, whole(low)), (w["gain"], whole(w["gain"])), (w["shift"], whole(w["shift"]))]
    ins += [(a, ANY) for a in (hat1, rstd1, w["back"], slope, w["in"], w["out"], ctx)]
    half = (ff + width) // 2
    outs = [(hbm_shape((half, width), BF), ANY)] * 2
    outs += [(s, whole(s)) for s in (shape((rows, width), BF), shape((rows, width), BF), shape((8, width), F32), shape((1, ff), F32))]
    scratch = [((rows, width), BF), ((rows, 128), F32), ((ff, width), BF), ((rows, ff), BF), ((width, ff), BF), ((width, width), BF), ((rows, width), BF)]
    scratch += [((rows, width), BF), ((rows, ff), BF), ((ff + width, width), BF)]
    scratch = [pltpu.VMEM(d, t) for d, t in scratch]
    scratch += [pltpu.SemaphoreType.DMA((5 + 2 * (ff // width),)), pltpu.SemaphoreType.DMA((8,))]
    return kernel_call(ff_back_body, "layer0_ff_back", (1,), ins, outs, 2 * rows * width * (3 * ff + 2 * width), scratch)


def attention_back_body(qkv_ref, prob_ref, dctx_ref, short_ref, long_ref, sums1_ref, sums2_ref, sumin_ref, dqkv_ref, keep_hbm, send_hbm, acc, sums, block, sent):
    step = pl.program_id(0)
    x = jnp.where(step == 0, short_ref[...], long_ref[...])
    rows, width = x.shape
    pair = 2 * width // HEADS
    first = first_head(width)
    scale = 1.0 / math.sqrt(width // HEADS)

    @pl.when(step == 0)
    def _():
        acc[...] = jnp.zeros_like(acc)
        sums[...] = jnp.zeros_like(sums)

    pairs = range(HEADS // 2)
    c = [[slice(m * width + p * pair, m * width + (p + 1) * pair) for m in range(3)] for p in pairs]
    for b in range(rows // BLOCK):
        r = slice(b * BLOCK, (b + 1) * BLOCK)
        dd = [halves(dctx_ref[r, c[p][0]], first) for p in pairs]
        dprob = [mm_nt(qkv_ref[r, c[p][2]], dd[p]) for p in pairs]
        dscore = []
        for p in pairs:
            prob = prob_ref[b, p].astype(F32)
            dscore.append((prob * (dprob[p] - jnp.sum(prob * dprob[p], 0, keepdims=True)) * scale).astype(BF))
        dv = [mm(prob_ref[b, p], dd[p]).astype(BF) for p in pairs]
        dk = [mm(dscore[p], halves(qkv_ref[r, c[p][0]], first)).astype(BF) for p in pairs]
        dq = [join_halves(mm_tn(dscore[p], qkv_ref[r, c[p][1]]), first).astype(BF) for p in pairs]
        dqkv_ref[r] = jnp.concatenate(dq + dk + dv, 1)
    dqkv = dqkv_ref[...]
    acc[...] += mm_tn(x, dqkv)
    sums[0:1] += rowsum(dqkv)

    @pl.when(step == pl.num_programs(0) - 1)
    def _():
        place = Halves(keep_hbm, send_hbm, block, sent)
        for m in range(3):
            place.put(m * width, acc[:, m * width : (m + 1) * width].astype(BF))
        rows_of = [sums[0:1, :width], sums[0:1, 2 * width :]]
        for k in range(3):
            rows_of += [sums1_ref[k : k + 1], sums2_ref[k : k + 1]]
        rows_of += [sumin_ref[:, k * width : (k + 1) * width] for k in range(sumin_ref.shape[1] // width)]
        rows_of += [sums2_ref[3:4], jnp.zeros((3, width), F32)]
        rows_of += [jnp.zeros((VECTOR_ROWS - 16, width), F32)]
        place.put(3 * width, jnp.concatenate(rows_of, 0).astype(BF))
        place.finish()


def attention_back(qkv, prob, dctx, sums1, sums2, sumin, short, long):
    rows, width = dctx.shape
    per = STEP // BLOCK
    ins = [(qkv, by_rows(3 * width)), (prob, pl.BlockSpec((per,) + prob.shape[1:], lambda i: (i, 0, 0, 0))), (dctx, by_rows(width))]
    ins += from_buckets(short, long) + [(a, whole(a)) for a in (sums1, sums2, sumin)]
    total = 3 * width + VECTOR_ROWS
    outs = [(hbm_shape((rows, 3 * width), BF), by_rows(3 * width))] + [(hbm_shape((total // 2, width), BF), ANY)] * 2
    scratch = [pltpu.VMEM((width, 3 * width), F32), pltpu.VMEM((8, 3 * width), F32), pltpu.VMEM((total, width), BF), pltpu.SemaphoreType.DMA((8,))]
    flops = 2 * rows * width * (3 * width + 10 * BLOCK)
    return kernel_call(attention_back_body, "layer0_attention_back", (rows // STEP,), ins, outs, flops, scratch)


def input_back_body(dqkv_ref, datt_ref, wqkv_ref, short_ref, long_ref):
    dx = datt_ref[...].astype(F32) + mm_nt(dqkv_ref[...], wqkv_ref[...])

    @pl.when(pl.program_id(0) == 0)
    def _():
        short_ref[...] = dx

    @pl.when(pl.program_id(0) > 0)
    def _():
        long_ref[...] = dx


def input_back(dqkv, datt, w, cut):
    rows, width = datt.shape
    ins = [(dqkv, by_rows(3 * width)), (datt, by_rows(width)), layer_of(w["qkv"], 0)]
    outs = [
        (shape((cut, width), F32), pl.BlockSpec((STEP, width), lambda i: (0, 0))),
        (shape((rows - cut, width), F32), pl.BlockSpec((STEP, width), lambda i: (jnp.maximum(i - 1, 0), 0))),
    ]
    return kernel_call(input_back_body, "layer0_input_back", (rows // STEP,), ins, outs, 2 * rows * width * 3 * width)


def unpack_call(body, name, bit, grid, ins, outs, aliases, size):
    return pl.pallas_call(
        body,
        grid_spec=pltpu.PrefetchScalarGridSpec(
            num_scalar_prefetch=1,
            grid=grid,
            in_specs=[s for _, s in ins],
            out_specs=[s for _, s in outs],
        ),
        out_shape=[s for s, _ in outs],
        input_output_aliases=aliases,
        compiler_params=pltpu.CompilerParams(vmem_limit_bytes=VMEM),
        cost_estimate=pl.CostEstimate(flops=0, bytes_accessed=size, transcendentals=0),
        name=name,
    )(bit, *[hbm(a) if s is ANY else a for a, s in ins])


def in_order(bit_ref, mine_ref, theirs_ref):
    mine, theirs = mine_ref[...].astype(F32), theirs_ref[...].astype(F32)
    low = bit_ref[0] == 0
    return jnp.where(low, mine, theirs), jnp.where(low, theirs, mine)


def unpack_first(bit, pair, back):
    _, ff, width = back.shape
    steps = ff // width
    block = pl.BlockSpec((width, width), lambda j, bit: (j, 0))

    def body(bit_ref, mine_ref, theirs_ref, _, qkv_ref, out_ref, back_ref):
        low, high = in_order(bit_ref, mine_ref, theirs_ref)
        back_ref[...] = low
        step = pl.program_id(0)

        @pl.when(step < steps - 1)
        def _():
            qkv_ref[...] = high

        @pl.when(step == steps - 1)
        def _():
            out_ref[...] = high

    outs = [
        (shape((2, width, 3 * width), F32), pl.BlockSpec((None, width, width), lambda j, bit: (1, 0, jnp.minimum(j, 2)))),
        (shape((2, width, width), F32), pl.BlockSpec((None, width, width), lambda j, bit: (1, 0, 0))),
        (shape(back.shape, F32), pl.BlockSpec((None, width, width), lambda j, bit: (0, j, 0))),
    ]
    ins = [(pair[0], block), (pair[1], block), (back, ANY)]
    return unpack_call(body, "unpack_first", bit, (steps,), ins, outs, {3: 2}, 12 * steps * width * width)


def unpack_second(bit, pair, gin, gout):
    _, width, ff = gin.shape
    rows = width // 2
    half = pair[0].shape[0] // rows
    count = 2 * ff // width
    block = [pl.BlockSpec((rows, width), lambda j, bit, low=low: (jnp.where((bit[0] == 0) == low, jnp.minimum(j, half - 1), jnp.maximum(j - half, 0)), 0)) for low in (True, False)]

    def body(bit_ref, mine_ref, theirs_ref, _, __, in_ref, out_ref):
        step = pl.program_id(0)
        mine = (step < half) == (bit_ref[0] == 0)
        value = jnp.where(mine, mine_ref[...], theirs_ref[...]).astype(F32)

        @pl.when(step < count)
        def _():
            in_ref[...] = value

        @pl.when(step >= count)
        def _():
            out_ref[...] = value

    def at_in(j, bit):
        j = jnp.minimum(j, count - 1)
        return 0, j % 2, j // 2

    outs = [
        (shape(gin.shape, F32), pl.BlockSpec((None, rows, width), at_in)),
        (shape(gout.shape, F32), pl.BlockSpec((None, rows, width), lambda j, bit: (0, jnp.maximum(j - count, 0), 0))),
    ]
    ins = [(pair[0], block[0]), (pair[1], block[1]), (gin, ANY), (gout, ANY)]
    return unpack_call(body, "unpack_second", bit, (2 * half,), ins, outs, {3: 0, 4: 1}, 12 * half * rows * width)


def unpack_third(bit, pair, qkv, sums, sumin):
    _, width, _ = qkv.shape
    ff = sumin.shape[1]
    total = 3 * width + VECTOR_ROWS

    def fixed(a):
        return pl.BlockSpec(a.shape, lambda j, bit: (0,) * len(a.shape))

    def body(bit_ref, mine_ref, theirs_ref, _, sums_ref, sumin_ref, qkv_ref, bqv_ref, bresid_ref, gain_ref, shift_ref, bin_ref):
        low, high = in_order(bit_ref, mine_ref, theirs_ref)
        value = jnp.concatenate([low, high], 0)
        for m in range(3):
            qkv_ref[:, m * width : (m + 1) * width] = value[m * width : (m + 1) * width]
        value = value[3 * width :]
        for ref, lower, upper in (
            (bqv_ref, (value[0:1], value[1:2]), (value[12:13], sums_ref[6:7])),
            (bresid_ref, (value[2:3], value[3:4]), (sums_ref[0:1], sums_ref[1:2])),
            (gain_ref, (value[4:5], value[5:6]), (sums_ref[2:3], sums_ref[3:4])),
            (shift_ref, (value[6:7], value[7:8]), (sums_ref[4:5], sums_ref[5:6])),
        ):
            for level, both in enumerate((lower, upper)):
                for k in range(2):
                    ref[level : level + 1, k * width : (k + 1) * width] = both[k]
        for k in range(ff // width):
            bin_ref[0:1, k * width : (k + 1) * width] = value[8 + k : 9 + k]
        bin_ref[1:2, :] = sumin_ref[...]

    outs = [(shape(qkv.shape, F32), pl.BlockSpec((None, width, 3 * width), lambda j, bit: (0, 0, 0)))]
    outs += [(s, fixed(s)) for s in [shape((2, 2 * width), F32)] * 4 + [shape((2, ff), F32)]]
    ins = [(pair[0], fixed(pair[0])), (pair[1], fixed(pair[1])), (qkv, ANY), (sums, fixed(sums)), (sumin, fixed(sumin))]
    return unpack_call(body, "unpack_third", bit, (1,), ins, outs, {3: 0}, 6 * total * width)


def top_rows(attended, pair_index, weights):
    w_qkv, b_qv, w_out, b_resid, gain, shift, w_in, b_in, w_back = weights
    rows, width = attended.shape
    pairs = rows // 2
    hat1, rstd1 = ln_stats(attended.astype(F32))
    normed = hat1 * gain[:width] + shift[:width]
    normed_low = normed.astype(BF)
    activ, slope = gelu_pair(mm(normed_low, w_in) + b_in)
    activ = activ.astype(BF)
    hat2, rstd2 = ln_stats(normed + mm(activ, w_back) + b_resid[width:])
    pooled = hat2 * gain[width:] + shift[width:]
    radius = lax.rsqrt(jnp.sum(pooled * pooled, -1, keepdims=True) + unit_eps)
    unit = pooled * radius
    unit_low = unit.astype(BF)
    src, tgt = unit_low[:pairs], unit_low[pairs:]
    positive = (pair_index[:, None] == jnp.arange(pairs)[None, :]).astype(F32)
    logits = logit_scale * (mm_nt(src, tgt) - margin * positive)

    def soft(axis):
        powers = jnp.exp(logits - jnp.max(logits, axis, keepdims=True))
        return powers / jnp.sum(powers, axis, keepdims=True)

    dscore = (0.5 * logit_scale * (soft(1) + soft(0) - 2.0 * positive)).astype(BF)
    dunit = jnp.concatenate([mm(dscore, tgt), mm_tn(dscore, src)], 0)
    dy = radius * (dunit - unit * jnp.sum(dunit * unit, -1, keepdims=True))
    dg2, dc2 = colsum(dy * hat2), colsum(dy)
    dmixed = ln_back(dy, hat2, rstd2, gain[width:])
    dmixed_low = dmixed.astype(BF)
    dhidden = (mm_nt(dmixed_low, w_back) * slope).astype(BF)
    dnormed = dmixed + mm_nt(dhidden, w_in)
    dg1, dc1 = colsum(dnormed * hat1), colsum(dnormed)
    datt = ln_back(dnormed, hat1, rstd1, gain[:width])
    datt_low = datt.astype(BF)
    dctx = mm_nt(datt_low, w_out).astype(BF)
    grads = (mm_tn(normed_low, dhidden), mm_tn(activ, dmixed_low))
    vectors = dict(
        bv=colsum(dctx),
        b_resid=jnp.concatenate([colsum(datt), colsum(dmixed)]),
        gain=jnp.concatenate([dg1, dg2]),
        shift=jnp.concatenate([dc1, dc2]),
        b_in=colsum(dhidden),
    )
    return datt, dctx, grads, vectors


def per_device(short_tokens, long_tokens, short_len, long_len, pair_index, *params):
    n = lax.axis_size("stream") * lax.axis_size("dp")
    index = lax.axis_index("stream") * lax.axis_size("dp") + lax.axis_index("dp")
    width = short_tokens.shape[-1]
    spans = (short_tokens.shape[2], long_tokens.shape[2])
    counts = (short_tokens.shape[1], long_tokens.shape[1])
    sents = sum(counts)
    w_qkv, b_qv, w_out, b_resid, gain, shift, w_in, b_in, w_back = params
    w_qkv, b_qv, w_out, b_resid, gain, shift, w_in, b_in, w_back = (hbm(p) for p in (w_qkv, b_qv, w_out, b_resid, gain, shift, w_in, b_in, w_back))
    w = dict(qkv=w_qkv, b_qv=b_qv, out=w_out, b_resid=b_resid, gain=gain, shift=shift, b_in=b_in, back=w_back) | {"in": w_in}
    short, long = hbm(short_tokens.reshape(-1, width)), hbm(long_tokens.reshape(-1, width))
    lens = jnp.concatenate([short_len.reshape(-1), long_len.reshape(-1)])
    lens_wide = jnp.repeat(lens, HEADS)[:, None]

    y, *far = forward(short, long, lens, w, spans[0], counts[0])
    qkv, prob, ctx, hat1, rstd1, act, slope, hat2, rstd2 = (hbm(a) for a in far)
    sent, *kept = ask(y, lens_wide, w, spans, sents)
    every = gather_rows(sent, n)
    one_kernel = n * sents <= 512
    if one_kernel:
        top_args = (index.reshape(1).astype(jnp.int32), every, pair_index[None, :])
    else:
        datt, dctx, top_g, top_vec = top_rows(every, pair_index, tuple(p[1] for p in params))
        top_args = tuple(lax.dynamic_slice_in_dim(v, index * sents, sents, 0) for v in (datt, dctx))
    bits = my_bits(n)
    bit = bits[0].reshape(1).astype(jnp.int32)

    keep, send, dlow, sums2, *dy_top = turn(top_args, y, [hbm(a) for a in kept], w, hat2, rstd2, act, spans, sents)
    first = Lane(sum_steps(keep, send, n, bits), n)
    keep, send, datt0, dctx0, sums1, sumin = stage([first], lambda *a: ff_back(*a, w), (dlow, hat1, rstd1, slope, ctx))
    second = Lane(sum_steps(keep, send, n, bits), n)
    dqkv, keep, send = stage([first, second], lambda *a: attention_back(*a, short, long), (qkv, prob, dctx0, sums1, sums2, sumin))
    third = Lane(sum_steps(keep, send, n, bits), n)
    lanes = [first, second, third]
    dshort, dlong = stage(lanes, lambda *a: input_back(*a, w, counts[0] * spans[0]), (hbm(dqkv), datt0))
    if one_kernel:
        gin1, gback1, top_sums, top_sumin = stage(lanes, lambda *a: top_grads(*a, w), (every, *dy_top))
    else:
        gin1, gback1 = (jnp.stack([g, g]) for g in top_g)
        rows_of = [top_vec[k].reshape(2, width) for k in ("b_resid", "gain", "shift")]
        top_sums = jnp.concatenate(rows_of + [top_vec["bv"][None], jnp.zeros((1, width), F32)], 0)
        top_sumin = top_vec["b_in"][None]
    while first.result is None:
        stage(lanes)
    g_qkv, g_out, g_back = stage(lanes, lambda *a: unpack_first(bit, *a), (first.result, gback1))
    while second.result is None:
        stage(lanes)
    g_in, g_out = stage(lanes, lambda *a: unpack_second(bit, *a), (second.result, gin1, g_out))
    while third.result is None:
        stage(lanes)
    g_qkv, g_bqv, g_bresid, g_gain, g_shift, g_bin = unpack_third(bit, third.result, g_qkv, top_sums, top_sumin)
    outs = (g_qkv, g_bqv, g_out, g_bresid, g_gain, g_shift, g_in, g_bin, g_back)
    return outs + (dshort.reshape((1, counts[0], spans[0], width)), dlong.reshape((1, counts[1], spans[1], width)))


def solution(mesh):
    split = P("stream", "dp", None, None)
    in_specs = (split, split, P("stream", "dp"), P("stream", "dp")) + (P(),) * 10
    out_specs = (P(),) * 9 + (split, split)
    return jax.shard_map(per_device, mesh=mesh, in_specs=in_specs, out_specs=out_specs, check_vma=False)
```

time: 253 us -> 225 us (0.89)
  Pallas kernels: 122 us -> 106 us
  other arithmetic: 15.1 us -> 4.18 us
  starting transfers between devices: 29.5 us -> 38.1 us
  local copies, waits for them, and re-layouts: 9.54 us -> 2.57 us
  waiting for transfers between devices: 73.8 us -> 69.5 us
    pallas_call x9 -> x7, Pallas kernels: 109 us -> 91.1 us  [kernel_call(): pl.pallas_call(body, grid=grid, in_specs=[s for _, s in ins], out_specs=[...]
    ppermute x21 -> x29, starting transfers between devices: 29.5 us -> 38.1 us  [swap(): lax.ppermute(value, AXES, [(i, i ^ (hop[1] if i & 1 else hop[0])) for i i...]
    convert_element_type x6 -> x3, other arithmetic: 7.46 us -> 0.28 us  [sum_steps(): cur = (keep.astype(F32) + got.astype(F32)).astype(BF)]
    dynamic_slice x6 -> x0, local copies, waits for them, and re-layouts: 4.59 us -> none  [sum_steps(): theirs = lax.dynamic_slice_in_dim(cur, (1 - bit) * half, half, 0)]
    ppermute x21 -> x29, waiting for transfers between devices: 73.8 us -> 69.5 us  [swap(): lax.ppermute(value, AXES, [(i, i ^ (hop[1] if i & 1 else hop[0])) for i i...]
    convert_element_type x4 -> x6, other arithmetic: 3.34 us -> 0.57 us  [sum_steps(): cur = (cur.astype(F32) + got.astype(F32)).astype(BF)]
    pallas_call x2 -> x9, Pallas kernels: 13.4 us -> 14.8 us  [unpack_call(): pl.pallas_call(body, grid_spec=pltpu.PrefetchScalarGridSpec(num_scalar_pr...]
  transfers between devices with their start and end apart: 21 -> 29, of which waited for: 14 -> 17; matrix products, arithmetic and copies ran while one was open for 0% -> 0% of each run, Pallas kernels for 27% -> 25%
where the time goes in v1:
time: 225 us; the launch traced here: 221 us
  Pallas kernels  106 us (47%)
  waiting for transfers between devices  69.5 us (31%)
  starting transfers between devices  38.1 us (17%)
  other arithmetic  4.18 us (2%)
  local copies, waits for them, and re-layouts  2.57 us (1%)
    pallas_call x7, Pallas kernels, kernel_call(): pl.pallas_call(body, grid=grid, in_specs=[s for _, s in ins], out_specs=[...  91.1 us
    ppermute x29, waiting for transfers between devices, swap(): lax.ppermute(value, AXES, [(i, i ^ (hop[1] if i & 1 else hop[0])) for i i...  69.5 us
    ppermute x29, starting transfers between devices, swap(): lax.ppermute(value, AXES, [(i, i ^ (hop[1] if i & 1 else hop[0])) for i i...  38.1 us
    pallas_call x9, Pallas kernels, unpack_call(): pl.pallas_call(body, grid_spec=pltpu.PrefetchScalarGridSpec(num_scalar_pr...  14.8 us
  transfers between devices with their start and end apart: 29, of which 17 were waited for; matrix products, arithmetic and copies ran while one was open for 0% of the time, Pallas kernels for 25%

profile of v1, /device:TPU:0, one launch (start us, length us, event | category | flops | bytes accessed | tf_op | source)
XLA Modules:
  0.0 221.5 jit_solution(14984564147201159278)
XLA Ops:
  1.6 21.7 %layer0_forward.1 = (bf16[1280,512]{1,0:T(8,128)(2,1)S(1)}, bf16[1280,1536]{1,0:T(8,128)(2,1)}, bf16[10,4,128,256]{3,2,1,0:T(8,128)(2,1)}, bf16[1280,512]{1,0:T(...) custom-call(s32[16]{0:T(128)S(1)} %pad_add_fusion.lens_ref, ...), custom_call_target="tpu_custom_call" | custom-call | flops 8053063680 | bytes 37535808 | tf_op jit(solution)/shard_map/layer0_forward/pallas_call | solution.py:90
  23.3 4.7 %layer1_ask.1 = (bf16[16,512]{1,0:T(8,128)(2,1)S(1)}, bf16[16,512]{1,0:T(8,128)(2,1)}, bf16[128,512]{1,0:T(8,128)(2,1)}, bf16[128,512]{1,0:T(8,128)(2,1)}, bf16[...) custom-call(bf16[1280,512]{1,0:T(8,128)(2,1)S(1)} %get-tuple-element.160.y_ref.refs_7_, ...), custom_call_target="tpu_custom_call" | custom-call | flops 536870912 | bytes 6275584 | tf_op jit(solution)/shard_map/layer1_ask/pallas_call | solution.py:90
  28.0 3.0 %collective-permute-start = (bf16[1,16,512]{2,1,0:T(8,128)(2,1)S(1)}, bf16[1,16,512]{2,1,0:T(8,128)(2,1)S(1)}, u32[]{:S(2)}, u32[]{:S(2)}) collective-permute-start(bf16[1,16,512]{2,1,0:T(8,128)(2,1)S(1)} %bitcast.54), channel_id=1, source_target_pairs={{0,2},{1,3},{2,0},{3,1},{4,6},{5,7},{6,4},{7,5},{8,10},{9,11},{10,... | collective-permute-start | bytes 49160 | tf_op jit(solution)/shard_map/ppermute | solution.py:115
  32.7 2.1 collective-permute-start.1
  34.8 1.9 collective-permute-done.1
  36.7 3.1 %collective-permute-start.2 = (bf16[4,16,512]{2,1,0:T(8,128)(2,1)S(1)}, bf16[4,16,512]{2,1,0:T(8,128)(2,1)S(1)}, u32[]{:S(2)}, u32[]{:S(2)}) collective-permute-start(bf16[4,16,512]{2,1,0:T(8,128)(2,1)S(1)} %bitcast.58), channel_id=1, source_target_pairs={{0,8},{1,9},{2,10},{3,11},{4,12},{5,13},{6,14},{7,15},{8,0},{9,1},... | collective-permute-start | bytes 196616 | tf_op jit(solution)/shard_map/ppermute | solution.py:115
  39.9 2.2 %collective-permute-done.2 = bf16[4,16,512]{2,1,0:T(8,128)(2,1)S(1)} collective-permute-done((bf16[4,16,512]{2,1,0:T(8,128)(2,1)S(1)}, bf16[4,16,512]{2,1,0:T(8,128)(2,1)S(1)}, u32[]{:S(2)}, u32[]{:S(2)}) %collective-permute-start.2) | collective-permute-done | bytes 65568 | tf_op jit(solution)/shard_map/ppermute | solution.py:115
  42.1 1.9 collective-permute-start.3
  44.0 3.2 %collective-permute-done.3 = bf16[8,16,512]{2,1,0:T(8,128)(2,1)S(1)} collective-permute-done((bf16[8,16,512]{2,1,0:T(8,128)(2,1)S(1)}, bf16[8,16,512]{2,1,0:T(8,128)(2,1)S(1)}, u32[]{:S(2)}, u32[]{:S(2)}) %collective-permute-start.3) | collective-permute-done | bytes 131104 | tf_op jit(solution)/shard_map/ppermute | solution.py:115
  49.0 19.0 %turn.1 = (bf16[2048,512]{1,0:T(8,128)(2,1)}, bf16[2048,512]{1,0:T(8,128)(2,1)}, bf16[1280,512]{1,0:T(8,128)(2,1)S(1)}, f32[8,512]{1,0:T(8,128)S(1)}, f32[512,512]{1,0:T(8,128)}) custom-call(bf16[128,512]{1,0:T(8,128)(2,1)} %get-tuple-element.161.refs_0_, bf16[128,512]{1,0:T(8,128)(2,1)} %get-tuple-element.162.refs_1_, ...), custom_call_target="tpu_custom_call" | custom-call | flops 5502926848 | bytes 28984324 | tf_op jit(solution)/shard_map/turn/pallas_call | solution.py:90
  68.2 15.6 %layer0_ff_back.1 = (bf16[1280,512]{1,0:T(8,128)(2,1)}, bf16[1280,512]{1,0:T(8,128)(2,1)}, bf16[1280,512]{1,0:T(8,128)(2,1)S(1)}, bf16[1280,512]{1,0:T(8,128)(2,...) custom-call(bf16[1280,512]{1,0:T(8,128)(2,1)S(1)} %get-tuple-element.178.low_ref, f32[2,1024]{1,0:T(2,128)} %gain_ref.5, ...), custom_call_target="tpu_custom_call" | custom-call | flops 9395240960 | bytes 24551424 | tf_op jit(solution)/shard_map/layer0_ff_back/pallas_call | solution.py:90
  89.8 11.8 %layer0_attention_back.1 = (bf16[1280,1536]{1,0:T(8,128)(2,1)}, bf16[832,512]{1,0:T(8,128)(2,1)}, bf16[832,512]{1,0:T(8,128)(2,1)}) custom-call(bf16[1280,1536]{1,0:T(8,128)(2,1)} %get-tuple-element.200.qkv_ref, bf16[10,4,128,256]{3,2,1,0:T(8,128)(2,1)} %get-tuple-element.201.prob_ref, bf16[1280,512]{1,0:T(8,128)(2,1)S(1)} %copy-done.11, ...), custom_call_target="tpu_custom_call" | custom-call | flops 3690987520 | bytes 14852096 | tf_op jit(solution)/shard_map/layer0_attention_back/pallas_call | solution.py:90
  103.8 1.9 collective-permute-start.9
  107.2 7.1 %layer0_input_back.1 = (f32[256,512]{1,0:T(8,128)}, f32[1024,512]{1,0:T(8,128)}) custom-call(bf16[1280,1536]{1,0:T(8,128)(2,1)} %get-tuple-element.222.dqkv_ref, bf16[1280,512]{1,0:T(8,128)(2,1)S(1)} %copy-done.7, bf16[2,512,1536]{2,1,0:T(8,128)(2,1)} %wqkv_ref.5), custom_call_target="tpu_custom_call" | custom-call | flops 2013265920 | bytes 11010048 | tf_op jit(solution)/shard_map/layer0_input_back/pallas_call | solution.py:90
  114.2 5.4 %collective-permute-done.8 = bf16[512,512]{1,0:T(8,128)(2,1)S(1)} collective-permute-done((bf16[512,512]{1,0:T(8,128)(2,1)S(1)}, bf16[512,512]{1,0:T(8,128)(2,1)S(1)}, u32[]{:S(2)}, u32[]{:S(2)}) %collective-permute-start.8) | collective-permute-done | bytes 524320 | tf_op jit(solution)/shard_map/ppermute | solution.py:115
  120.8 2.0 collective-permute-start.11
  125.5 11.1 %top_grads.1 = (f32[2,512,2048]{2,1,0:T(8,128)}, f32[2,2048,512]{2,1,0:T(8,128)}, f32[8,512]{1,0:T(8,128)S(1)}, f32[1,2048]{1,0:T(1,128)S(1)}) custom-call(bf16[512,512]{1,0:T(8,128)(2,1)S(1)} %bitcast.53, f32[512,512]{1,0:T(8,128)S(1)} %copy-done.9, bf16[2,512,512]{2,1,0:T(8,128)(2,1)} %wout_ref.5, bf16[2,512,2048]{2,1,0:T(8,128)(2,1)} %win_ref.3, ...), custom_call_target="tpu_custom_call" | custom-call | flops 7247757312 | bytes 27860992 | tf_op jit(solution)/shard_map/top_grads/pallas_call | solution.py:90
  136.9 3.7 %collective-permute-start.14 = (bf16[512,512]{1,0:T(8,128)(2,1)S(1)}, bf16[512,512]{1,0:T(8,128)(2,1)S(1)}, u32[]{:S(2)}, u32[]{:S(2)}) collective-permute-start(bf16[512,512]{1,0:T(8,128)(2,1)S(1)} %add_convert_fusion.1), channel_id=1, source_target_pairs={{0,12},{1,5},{2,14},{3,7},{4,8},{5,1},{6,10},{7,3},{8,4},{9,13},{1... | collective-permute-start | bytes 1572872 | tf_op jit(solution)/shard_map/ppermute | solution.py:115
  141.8 4.7 %collective-permute-done.16 = bf16[208,512]{1,0:T(8,128)(2,1)S(1)} collective-permute-done((bf16[208,512]{1,0:T(8,128)(2,1)S(1)}, bf16[208,512]{1,0:T(8,128)(2,1)S(1)}, u32[]{:S(2)}, u32[]{:S(2)}) %collective-permute-start.16) | collective-permute-done | bytes 213024 | tf_op jit(solution)/shard_map/ppermute | solution.py:115
  146.6 12.9 %collective-permute-done.15 = bf16[320,512]{1,0:T(8,128)(2,1)S(1)} collective-permute-done((bf16[320,512]{1,0:T(8,128)(2,1)S(1)}, bf16[320,512]{1,0:T(8,128)(2,1)S(1)}, u32[]{:S(2)}, u32[]{:S(2)}) %collective-permute-start.15) | collective-permute-done | bytes 327712 | tf_op jit(solution)/shard_map/ppermute | solution.py:115
  163.0 11.3 %collective-permute-done.19 = bf16[208,512]{1,0:T(8,128)(2,1)S(1)} collective-permute-done((bf16[208,512]{1,0:T(8,128)(2,1)S(1)}, bf16[208,512]{1,0:T(8,128)(2,1)S(1)}, u32[]{:S(2)}, u32[]{:S(2)}) %collective-permute-start.19) | collective-permute-done | bytes 213024 | tf_op jit(solution)/shard_map/ppermute | solution.py:115
  177.2 2.2 collective-permute-start.22
  179.4 5.6 %collective-permute-done.22 = bf16[208,512]{1,0:T(8,128)(2,1)S(1)} collective-permute-done((bf16[208,512]{1,0:T(8,128)(2,1)S(1)}, bf16[208,512]{1,0:T(8,128)(2,1)S(1)}, u32[]{:S(2)}, u32[]{:S(2)}) %collective-permute-start.22) | collective-permute-done | bytes 213024 | tf_op jit(solution)/shard_map/ppermute | solution.py:115
  184.9 2.9 %collective-permute-done.21 = bf16[320,512]{1,0:T(8,128)(2,1)S(1)} collective-permute-done((bf16[320,512]{1,0:T(8,128)(2,1)S(1)}, bf16[320,512]{1,0:T(8,128)(2,1)S(1)}, u32[]{:S(2)}, u32[]{:S(2)}) %collective-permute-start.21) | collective-permute-done | bytes 327712 | tf_op jit(solution)/shard_map/ppermute | solution.py:115
  187.8 3.9 %collective-permute-done.20 = bf16[1024,512]{1,0:T(8,128)(2,1)S(1)} collective-permute-done((bf16[1024,512]{1,0:T(8,128)(2,1)}, bf16[1024,512]{1,0:T(8,128)(2,1)S(1)}, u32[]{:S(2)}, u32[]{:S(2)}) %collective-permute-start.20) | collective-permute-done | bytes 1048608 | tf_op jit(solution)/shard_map/ppermute | solution.py:115
  192.5 1.8 collective-permute-start.24
  196.1 6.5 %collective-permute-done.25 = bf16[208,512]{1,0:T(8,128)(2,1)S(1)} collective-permute-done((bf16[208,512]{1,0:T(8,128)(2,1)S(1)}, bf16[208,512]{1,0:T(8,128)(2,1)S(1)}, u32[]{:S(2)}, u32[]{:S(2)}) %collective-permute-start.25) | collective-permute-done | bytes 213024 | tf_op jit(solution)/shard_map/ppermute | solution.py:115
  202.5 2.9 %collective-permute-done.24 = bf16[640,512]{1,0:T(8,128)(2,1)S(1)} collective-permute-done((bf16[640,512]{1,0:T(8,128)(2,1)S(1)}, bf16[640,512]{1,0:T(8,128)(2,1)S(1)}, u32[]{:S(2)}, u32[]{:S(2)}) %collective-permute-start.24) | collective-permute-done | bytes 655392 | tf_op jit(solution)/shard_map/ppermute | solution.py:115
  207.8 4.0 %unpack_first.1 = (f32[2,512,1536]{2,1,0:T(8,128)}, f32[2,512,512]{2,1,0:T(8,128)}, f32[2,2048,512]{2,1,0:T(8,128)}) custom-call(s32[1]{0:T(128)} %bitcast.bit_ref, bf16[2048,512]{1,0:T(8,128)(2,1)S(1)} %pad_maximum_fusion.mine_ref, bf16[2048,512]{1,0:T(8,128)(2,1)S(1)} %collective-permute-done.23.theirs_ref, ...), custom_call_target="tpu_custom_call", output_to_operand_aliasing={{2}: (3, {})} | custom-call | bytes 12582912 | tf_op jit(solution)/shard_map/unpack_first/pallas_call | solution.py:750
  211.8 2.3 %collective-permute-done.27 = bf16[416,512]{1,0:T(8,128)(2,1)S(1)} collective-permute-done((bf16[416,512]{1,0:T(8,128)(2,1)S(1)}, bf16[416,512]{1,0:T(8,128)(2,1)S(1)}, u32[]{:S(2)}, u32[]{:S(2)}) %collective-permute-start.27) | collective-permute-done | bytes 426016 | tf_op jit(solution)/shard_map/ppermute | solution.py:115
  214.5 4.7 %unpack_second.1 = (f32[2,512,2048]{2,1,0:T(8,128)}, f32[2,512,512]{2,1,0:T(8,128)}) custom-call(s32[1]{0:T(128)} %bitcast.bit_ref, bf16[1280,512]{1,0:T(8,128)(2,1)S(1)} %pad_maximum_fusion.1.mine_ref, bf16[1280,512]{1,0:T(8,128)(2,1)S(1)} %collective-permute-done.26.theirs_ref, ...), custom_call_target="tpu_custom_call", output_to_operand_aliasing={{0}: (3, {}), {1}: (4, {})} | custom-call | bytes 7864320 | tf_op jit(solution)/shard_map/unpack_second/pallas_call | solution.py:750
  219.2 2.1 unpack_third.1
  (102 shorter events, 31.0 us)
Async XLA Ops:
  28.0 4.7 %collective-permute-start = (bf16[1,16,512]{2,1,0:T(8,128)(2,1)S(1)}, bf16[1,16,512]{2,1,0:T(8,128)(2,1)S(1)}, u32[]{:S(2)}, u32[]{:S(2)}) collective-permute-start(bf16[1,16,512]{2,1,0:T(8,128)(2,1)S(1)} %bitcast.54), channel_id=1, source_target_pairs={{0,2},{1,3},{2,0},{3,1},{4,6},{5,7},{6,4},{7,5},{8,10},{9,11},{10,... | collective-permute-start | bytes 49160 | tf_op jit(solution)/shard_map/ppermute | solution.py:115
  32.7 4.0 %collective-permute-start.1 = (bf16[2,16,512]{2,1,0:T(8,128)(2,1)S(1)}, bf16[2,16,512]{2,1,0:T(8,128)(2,1)S(1)}, u32[]{:S(2)}, u32[]{:S(2)}) collective-permute-start(bf16[2,16,512]{2,1,0:T(8,128)(2,1)S(1)} %maximum_bitcast_fusion), channel_id=1, source_target_pairs={{0,4},{1,5},{2,6},{3,7},{4,0},{5,1},{6,2},{7,3},{8,12},{9,13},{10,... | collective-permute-start | bytes 98312 | tf_op jit(solution)/shard_map/ppermute | solution.py:115
  36.7 5.4 %collective-permute-start.2 = (bf16[4,16,512]{2,1,0:T(8,128)(2,1)S(1)}, bf16[4,16,512]{2,1,0:T(8,128)(2,1)S(1)}, u32[]{:S(2)}, u32[]{:S(2)}) collective-permute-start(bf16[4,16,512]{2,1,0:T(8,128)(2,1)S(1)} %bitcast.58), channel_id=1, source_target_pairs={{0,8},{1,9},{2,10},{3,11},{4,12},{5,13},{6,14},{7,15},{8,0},{9,1},... | collective-permute-start | bytes 196616 | tf_op jit(solution)/shard_map/ppermute | solution.py:115
  42.1 5.0 %collective-permute-start.3 = (bf16[8,16,512]{2,1,0:T(8,128)(2,1)S(1)}, bf16[8,16,512]{2,1,0:T(8,128)(2,1)S(1)}, u32[]{:S(2)}, u32[]{:S(2)}) collective-permute-start(bf16[8,16,512]{2,1,0:T(8,128)(2,1)S(1)} %bitcast.57), channel_id=1, source_target_pairs={{0,16},{1,17},{2,18},{3,19},{4,20},{5,21},{6,22},{7,23},{8,24},{9,... | collective-permute-start | bytes 393224 | tf_op jit(solution)/shard_map/ppermute | solution.py:115
  47.3 1.6 collective-permute-start.4
  49.0 19.1 %copy-start.4 = (bf16[16,2,16,512]{3,2,1,0:T(8,128)(2,1)}, bf16[16,2,16,512]{3,2,1,0:T(8,128)(2,1)S(1)}, u32[]{:S(2)}) copy-start(bf16[16,2,16,512]{3,2,1,0:T(8,128)(2,1)S(1)} %pad_maximum_fusion.5) | copy-start | bytes 1572868
  68.0 16.9 %collective-permute-start.5 = (bf16[2048,512]{1,0:T(8,128)(2,1)}, bf16[2048,512]{1,0:T(8,128)(2,1)S(1)}, u32[]{:S(2)}, u32[]{:S(2)}) collective-permute-start(bf16[2048,512]{1,0:T(8,128)(2,1)} %get-tuple-element.177), channel_id=1, source_target_pairs={{0,1},{1,0},{2,3},{3,2},{4,5},{5,4},{6,7},{7,6},{8,9},{9,8},{10,11... | collective-permute-start | bytes 6291464 | tf_op jit(solution)/shard_map/ppermute | solution.py:115
  68.2 16.7 %copy-start = (bf16[2048,512]{1,0:T(8,128)(2,1)S(1)}, bf16[2048,512]{1,0:T(8,128)(2,1)}, u32[]{:S(2)}) copy-start(bf16[2048,512]{1,0:T(8,128)(2,1)} %get-tuple-element.170.mine_a.mine_b) | copy-start | bytes 6291460
  86.3 15.5 %collective-permute-start.7 = (bf16[1280,512]{1,0:T(8,128)(2,1)}, bf16[1280,512]{1,0:T(8,128)(2,1)S(1)}, u32[]{:S(2)}, u32[]{:S(2)}) collective-permute-start(bf16[1280,512]{1,0:T(8,128)(2,1)} %get-tuple-element.199), channel_id=1, source_target_pairs={{0,1},{1,0},{2,3},{3,2},{4,5},{5,4},{6,7},{7,6},{8,9},{9,8},{10,11... | collective-permute-start | bytes 3932168 | tf_op jit(solution)/shard_map/ppermute | solution.py:115
  86.7 15.1 %collective-permute-start.6 = (bf16[1024,512]{1,0:T(8,128)(2,1)}, bf16[1024,512]{1,0:T(8,128)(2,1)}, u32[]{:S(2)}, u32[]{:S(2)}) collective-permute-start(bf16[1024,512]{1,0:T(8,128)(2,1)} %get-tuple-element.198), channel_id=1, source_target_pairs={{0,16},{1,3},{2,18},{3,1},{4,20},{5,7},{6,22},{7,5},{8,24},{9,11},... | collective-permute-start | bytes 3145736 | tf_op jit(solution)/shard_map/ppermute | solution.py:115
  103.7 16.4 %copy-start.3 = (bf16[832,512]{1,0:T(8,128)(2,1)S(1)}, bf16[832,512]{1,0:T(8,128)(2,1)}, u32[]{:S(2)}) copy-start(bf16[832,512]{1,0:T(8,128)(2,1)} %get-tuple-element.209.mine_a.mine_b) | copy-start | bytes 2555908
  103.7 16.4 %collective-permute-start.10 = (bf16[832,512]{1,0:T(8,128)(2,1)S(1)}, bf16[832,512]{1,0:T(8,128)(2,1)S(1)}, u32[]{:S(2)}, u32[]{:S(2)}) collective-permute-start(bf16[832,512]{1,0:T(8,128)(2,1)S(1)} %copy-done.12), channel_id=1, source_target_pairs={{0,1},{1,0},{2,3},{3,2},{4,5},{5,4},{6,7},{7,6},{8,9},{9,8},{10,11... | collective-permute-start | bytes 2555912 | tf_op jit(solution)/shard_map/ppermute | solution.py:115
  103.8 16.3 %collective-permute-start.9 = (bf16[640,512]{1,0:T(8,128)(2,1)S(1)}, bf16[640,512]{1,0:T(8,128)(2,1)S(1)}, u32[]{:S(2)}, u32[]{:S(2)}) collective-permute-start(bf16[640,512]{1,0:T(8,128)(2,1)S(1)} %get-tuple-element.220), channel_id=1, source_target_pairs={{0,16},{1,3},{2,18},{3,1},{4,20},{5,7},{6,22},{7,5},{8,24},{9,11},... | collective-permute-start | bytes 1966088 | tf_op jit(solution)/shard_map/ppermute | solution.py:115
  105.6 14.0 %collective-permute-start.8 = (bf16[512,512]{1,0:T(8,128)(2,1)S(1)}, bf16[512,512]{1,0:T(8,128)(2,1)S(1)}, u32[]{:S(2)}, u32[]{:S(2)}) collective-permute-start(bf16[512,512]{1,0:T(8,128)(2,1)S(1)} %get-tuple-element.219), channel_id=1, source_target_pairs={{0,2},{1,17},{2,0},{3,19},{4,6},{5,21},{6,4},{7,23},{8,10},{9,25},... | collective-permute-start | bytes 1572872 | tf_op jit(solution)/shard_map/ppermute | solution.py:115
  120.8 15.7 %collective-permute-start.11 = (bf16[512,512]{1,0:T(8,128)(2,1)S(1)}, bf16[512,512]{1,0:T(8,128)(2,1)S(1)}, u32[]{:S(2)}, u32[]{:S(2)}) collective-permute-start(bf16[512,512]{1,0:T(8,128)(2,1)S(1)} %add_convert_fusion.2), channel_id=1, source_target_pairs={{0,4},{1,13},{2,6},{3,15},{4,0},{5,9},{6,2},{7,11},{8,12},{9,5},{1... | collective-permute-start | bytes 1572872 | tf_op jit(solution)/shard_map/ppermute | solution.py:115
  122.8 13.8 %collective-permute-start.13 = (bf16[416,512]{1,0:T(8,128)(2,1)S(1)}, bf16[416,512]{1,0:T(8,128)(2,1)S(1)}, u32[]{:S(2)}, u32[]{:S(2)}) collective-permute-start(bf16[416,512]{1,0:T(8,128)(2,1)S(1)} %get-tuple-element.237), channel_id=1, source_target_pairs={{0,16},{1,3},{2,18},{3,1},{4,20},{5,7},{6,22},{7,5},{8,24},{9,11},... | collective-permute-start | bytes 1277960 | tf_op jit(solution)/shard_map/ppermute | solution.py:115
  124.3 12.3 %collective-permute-start.12 = (bf16[320,512]{1,0:T(8,128)(2,1)S(1)}, bf16[320,512]{1,0:T(8,128)(2,1)S(1)}, u32[]{:S(2)}, u32[]{:S(2)}) collective-permute-start(bf16[320,512]{1,0:T(8,128)(2,1)S(1)} %get-tuple-element.236), channel_id=1, source_target_pairs={{0,2},{1,17},{2,0},{3,19},{4,6},{5,21},{6,4},{7,23},{8,10},{9,25},... | collective-permute-start | bytes 983048 | tf_op jit(solution)/shard_map/ppermute | solution.py:115
  136.9 22.6 %collective-permute-start.14 = (bf16[512,512]{1,0:T(8,128)(2,1)S(1)}, bf16[512,512]{1,0:T(8,128)(2,1)S(1)}, u32[]{:S(2)}, u32[]{:S(2)}) collective-permute-start(bf16[512,512]{1,0:T(8,128)(2,1)S(1)} %add_convert_fusion.1), channel_id=1, source_target_pairs={{0,12},{1,5},{2,14},{3,7},{4,8},{5,1},{6,10},{7,3},{8,4},{9,13},{1... | collective-permute-start | bytes 1572872 | tf_op jit(solution)/shard_map/ppermute | solution.py:115
  140.6 18.9 %collective-permute-start.15 = (bf16[320,512]{1,0:T(8,128)(2,1)S(1)}, bf16[320,512]{1,0:T(8,128)(2,1)S(1)}, u32[]{:S(2)}, u32[]{:S(2)}) collective-permute-start(bf16[320,512]{1,0:T(8,128)(2,1)S(1)} %add_convert_fusion.5), channel_id=1, source_target_pairs={{0,4},{1,13},{2,6},{3,15},{4,0},{5,9},{6,2},{7,11},{8,12},{9,5},{1... | collective-permute-start | bytes 983048 | tf_op jit(solution)/shard_map/ppermute | solution.py:115
  140.7 5.8 %collective-permute-start.16 = (bf16[208,512]{1,0:T(8,128)(2,1)S(1)}, bf16[208,512]{1,0:T(8,128)(2,1)S(1)}, u32[]{:S(2)}, u32[]{:S(2)}) collective-permute-start(bf16[208,512]{1,0:T(8,128)(2,1)S(1)} %get-tuple-element.252), channel_id=1, source_target_pairs={{0,2},{1,17},{2,0},{3,19},{4,6},{5,21},{6,4},{7,23},{8,10},{9,25},... | collective-permute-start | bytes 638984 | tf_op jit(solution)/shard_map/ppermute | solution.py:115
  159.8 14.4 %collective-permute-start.17 = (bf16[512,512]{1,0:T(8,128)(2,1)S(1)}, bf16[512,512]{1,0:T(8,128)(2,1)S(1)}, u32[]{:S(2)}, u32[]{:S(2)}) collective-permute-start(bf16[512,512]{1,0:T(8,128)(2,1)S(1)} %add_convert_fusion), channel_id=1, source_target_pairs={{0,2},{1,17},{2,0},{3,19},{4,6},{5,21},{6,4},{7,23},{8,10},{9,25},... | collective-permute-start | bytes 1572872 | tf_op jit(solution)/shard_map/ppermute | solution.py:115
  160.4 13.9 %collective-permute-start.18 = (bf16[320,512]{1,0:T(8,128)(2,1)S(1)}, bf16[320,512]{1,0:T(8,128)(2,1)S(1)}, u32[]{:S(2)}, u32[]{:S(2)}) collective-permute-start(bf16[320,512]{1,0:T(8,128)(2,1)S(1)} %add_convert_fusion.4), channel_id=1, source_target_pairs={{0,12},{1,5},{2,14},{3,7},{4,8},{5,1},{6,10},{7,3},{8,4},{9,13},{1... | collective-permute-start | bytes 983048 | tf_op jit(solution)/shard_map/ppermute | solution.py:115
  162.1 12.2 %collective-permute-start.19 = (bf16[208,512]{1,0:T(8,128)(2,1)S(1)}, bf16[208,512]{1,0:T(8,128)(2,1)S(1)}, u32[]{:S(2)}, u32[]{:S(2)}) collective-permute-start(bf16[208,512]{1,0:T(8,128)(2,1)S(1)} %add_convert_fusion.8), channel_id=1, source_target_pairs={{0,4},{1,13},{2,6},{3,15},{4,0},{5,9},{6,2},{7,11},{8,12},{9,5},{1... | collective-permute-start | bytes 638984 | tf_op jit(solution)/shard_map/ppermute | solution.py:115
  175.5 16.2 %collective-permute-start.20 = (bf16[1024,512]{1,0:T(8,128)(2,1)}, bf16[1024,512]{1,0:T(8,128)(2,1)S(1)}, u32[]{:S(2)}, u32[]{:S(2)}) collective-permute-start(bf16[1024,512]{1,0:T(8,128)(2,1)} %pad_maximum_fusion.2), channel_id=1, source_target_pairs={{0,16},{1,3},{2,18},{3,1},{4,20},{5,7},{6,22},{7,5},{8,24},{9,11},... | collective-permute-start | bytes 3145736 | tf_op jit(solution)/shard_map/ppermute | solution.py:115
  177.2 10.7 %collective-permute-start.21 = (bf16[320,512]{1,0:T(8,128)(2,1)S(1)}, bf16[320,512]{1,0:T(8,128)(2,1)S(1)}, u32[]{:S(2)}, u32[]{:S(2)}) collective-permute-start(bf16[320,512]{1,0:T(8,128)(2,1)S(1)} %add_convert_fusion.3), channel_id=1, source_target_pairs={{0,2},{1,17},{2,0},{3,19},{4,6},{5,21},{6,4},{7,23},{8,10},{9,25},... | collective-permute-start | bytes 983048 | tf_op jit(solution)/shard_map/ppermute | solution.py:115
  177.2 7.7 %collective-permute-start.22 = (bf16[208,512]{1,0:T(8,128)(2,1)S(1)}, bf16[208,512]{1,0:T(8,128)(2,1)S(1)}, u32[]{:S(2)}, u32[]{:S(2)}) collective-permute-start(bf16[208,512]{1,0:T(8,128)(2,1)S(1)} %add_convert_fusion.7), channel_id=1, source_target_pairs={{0,12},{1,5},{2,14},{3,7},{4,8},{5,1},{6,10},{7,3},{8,4},{9,13},{1... | collective-permute-start | bytes 638984 | tf_op jit(solution)/shard_map/ppermute | solution.py:115
  192.4 13.0 %collective-permute-start.23 = (bf16[2048,512]{1,0:T(8,128)(2,1)S(1)}, bf16[2048,512]{1,0:T(8,128)(2,1)S(1)}, u32[]{:S(2)}, u32[]{:S(2)}) collective-permute-start(bf16[2048,512]{1,0:T(8,128)(2,1)S(1)} %pad_maximum_fusion.mine_ref), channel_id=1, source_target_pairs={{0,1},{1,0},{2,3},{3,2},{4,5},{5,4},{6,7},{7,6},{8,9},{9,8},{10,11... | collective-permute-start | bytes 6291464 | tf_op jit(solution)/shard_map/ppermute | solution.py:115
  192.5 12.9 %collective-permute-start.24 = (bf16[640,512]{1,0:T(8,128)(2,1)S(1)}, bf16[640,512]{1,0:T(8,128)(2,1)S(1)}, u32[]{:S(2)}, u32[]{:S(2)}) collective-permute-start(bf16[640,512]{1,0:T(8,128)(2,1)S(1)} %pad_maximum_fusion.4), channel_id=1, source_target_pairs={{0,16},{1,3},{2,18},{3,1},{4,20},{5,7},{6,22},{7,5},{8,24},{9,11},... | collective-permute-start | bytes 1966088 | tf_op jit(solution)/shard_map/ppermute | solution.py:115
  194.3 8.2 %collective-permute-start.25 = (bf16[208,512]{1,0:T(8,128)(2,1)S(1)}, bf16[208,512]{1,0:T(8,128)(2,1)S(1)}, u32[]{:S(2)}, u32[]{:S(2)}) collective-permute-start(bf16[208,512]{1,0:T(8,128)(2,1)S(1)} %add_convert_fusion.6), channel_id=1, source_target_pairs={{0,2},{1,17},{2,0},{3,19},{4,6},{5,21},{6,4},{7,23},{8,10},{9,25},... | collective-permute-start | bytes 638984 | tf_op jit(solution)/shard_map/ppermute | solution.py:115
  205.9 8.3 %collective-permute-start.26 = (bf16[1280,512]{1,0:T(8,128)(2,1)S(1)}, bf16[1280,512]{1,0:T(8,128)(2,1)S(1)}, u32[]{:S(2)}, u32[]{:S(2)}) collective-permute-start(bf16[1280,512]{1,0:T(8,128)(2,1)S(1)} %pad_maximum_fusion.1.mine_ref), channel_id=1, source_target_pairs={{0,1},{1,0},{2,3},{3,2},{4,5},{5,4},{6,7},{7,6},{8,9},{9,8},{10,11... | collective-permute-start | bytes 3932168 | tf_op jit(solution)/shard_map/ppermute | solution.py:115
  205.9 8.2 %collective-permute-start.27 = (bf16[416,512]{1,0:T(8,128)(2,1)S(1)}, bf16[416,512]{1,0:T(8,128)(2,1)S(1)}, u32[]{:S(2)}, u32[]{:S(2)}) collective-permute-start(bf16[416,512]{1,0:T(8,128)(2,1)S(1)} %pad_maximum_fusion.6), channel_id=1, source_target_pairs={{0,16},{1,3},{2,18},{3,1},{4,20},{5,7},{6,22},{7,5},{8,24},{9,11},... | collective-permute-start | bytes 1277960 | tf_op jit(solution)/shard_map/ppermute | solution.py:115
  214.4 4.8 %collective-permute-start.28 = (bf16[832,512]{1,0:T(8,128)(2,1)S(1)}, bf16[832,512]{1,0:T(8,128)(2,1)S(1)}, u32[]{:S(2)}, u32[]{:S(2)}) collective-permute-start(bf16[832,512]{1,0:T(8,128)(2,1)S(1)} %pad_maximum_fusion.3.mine_ref), channel_id=1, source_target_pairs={{0,1},{1,0},{2,3},{3,2},{4,5},{5,4},{6,7},{7,6},{8,9},{9,8},{10,11... | collective-permute-start | bytes 2555912 | tf_op jit(solution)/shard_map/ppermute | solution.py:115
  (10 other events, 53.8 us)
